TPU v7x, 512 devices: a whole 4x4x16 slice. The times are simulated.
512 devices in a mesh: dp: 64 (over x, z_lo, core), tensor: 8 (over z_hi, y).
Axes of the slice: x: 4, y: 4, z: 16 (z_hi: 2, z_lo: 8; z = z_hi * 8 + z_lo), core: 2. Of those that a mesh axis runs over, the one named last changes fastest.
Arguments:
- query_heads: bfloat16 [32768, 8192], P('dp', 'tensor'), may hold values from -165 to 165
- key_heads: bfloat16 [32768, 1024], P('dp', 'tensor'), may hold values from -6 to 6
- value_heads: bfloat16 [32768, 1024], P('dp', 'tensor'), may hold values from -6 to 6
- logp_grad: bfloat16 [32768, 8192], P('dp', 'tensor'), may hold values from -6 to 6
- logp_new: float32 [32768], P(('dp', 'tensor')), may hold values from -3 to 0
- logp_old: float32 [32768], P(('dp', 'tensor')), may hold values from -3 to 0
- advantage: float32 [32768], P(('dp', 'tensor')), may hold values from -6 to 6
- ratio_caps: float32 [4], replicated, may hold values from 1.05 to 2
- live_counts: int32 [64], P('dp'), may hold values from 0 to 512, as said below
- seq_begin: int32 [32768], P('dp'), may hold values from 0 to 511, as said below
- seg_begin: int32 [32768], P('dp'), may hold values from 0 to 511, as said below
- policy_version: int32 [32768], P('dp'), may hold values from 0 to 3, as said below
Outputs:
- grad_queries: bfloat16 [32768, 8192], P('dp', 'tensor')
- grad_keys: bfloat16 [32768, 1024], P('dp', 'tensor')
- grad_values: bfloat16 [32768, 1024], P('dp', 'tensor')
Inputs may be any that keep to these rules, and one draw needn't show every extreme that they name: `live_counts`: rows of a block from its count on are padding. `seq_begin`: given as a row of the block (0 to 511); each sequence is a run of consecutive rows that begins at that row; every padding row is a sequence of its own. `seg_begin`: given as a row of the block; segments are runs of consecutive rows inside one sequence, and every sequence begins a segment. `policy_version`: all rows of a segment share one version.
All inputs are finite; a program needn't handle non-finite values.
Results may differ from a plain program's by a relative error of at most 0.017.
Values may be sent and summed in bfloat16 or wider, within the bound.
A program may use at most 64 MiB of HBM per device.

v0:
```python
import jax
import jax.numpy as jnp
from jax import lax
from jax.sharding import PartitionSpec as P

HEAD_DIM = 128
KEY_BLOCK = 128


def for_sending(array):
    return jax.tree.map(lambda a: a.astype(jnp.bfloat16) if a.dtype == jnp.float32 else a, array)


def swapped(array, axis, bit):
    return lax.ppermute(array, axis, [(i, i ^ 1 << bit) for i in range(lax.axis_size(axis))])


def attend_grad(query_heads, key_heads, value_heads, d_out, seq_begin, query_rows, block_count):
    row_total, columns = query_heads.shape
    kv_heads = key_heads.shape[1] // HEAD_DIM
    groups = columns // key_heads.shape[1]
    score_scale = HEAD_DIM ** (-0.5)
    q_grouped = query_heads.reshape(row_total, kv_heads, groups, HEAD_DIM)
    d_grouped = d_out.reshape(row_total, kv_heads, groups, HEAD_DIM)
    k_grouped = key_heads.reshape(row_total, kv_heads, HEAD_DIM)
    v_grouped = value_heads.reshape(row_total, kv_heads, HEAD_DIM)

    def tile_pair(query_block, key_block_id):
        query_first = query_block * KEY_BLOCK
        key_first = key_block_id * KEY_BLOCK
        q_tile = lax.dynamic_slice_in_dim(q_grouped, query_first, KEY_BLOCK, 0)
        d_tile = lax.dynamic_slice_in_dim(d_grouped, query_first, KEY_BLOCK, 0)
        begin_tile = lax.dynamic_slice_in_dim(seq_begin, query_first, KEY_BLOCK, 0)
        row_tile = lax.dynamic_slice_in_dim(query_rows, query_first, KEY_BLOCK, 0)
        key_tile = lax.dynamic_slice_in_dim(k_grouped, key_first, KEY_BLOCK, 0)
        value_tile = lax.dynamic_slice_in_dim(v_grouped, key_first, KEY_BLOCK, 0)
        key_rows = key_first + jnp.arange(KEY_BLOCK, dtype=jnp.int32)
        allowed = (key_rows[None, :] >= begin_tile[:, None]) & (
            key_rows[None, :] <= row_tile[:, None]
        )
        scores = (
            jnp.einsum("tkgd,jkd->kgtj", q_tile, key_tile, preferred_element_type=jnp.float32)
            * score_scale
        )
        d_prob = jnp.einsum(
            "tkgd,jkd->kgtj", d_tile, value_tile, preferred_element_type=jnp.float32
        )
        return (q_tile, d_tile, key_tile, allowed, scores, d_prob)

    def stats_tile(query_block, arrays):
        top_all, mass_all, wsum_all = arrays

        def stats_visit(key_block_id, carry):
            row_top, row_mass, row_wsum = carry
            q_tile, d_tile, key_tile, allowed, scores, d_prob = tile_pair(query_block, key_block_id)
            masked = jnp.where(allowed, scores, -1e30)
            new_top = jnp.maximum(row_top, jnp.max(masked, axis=-1))
            rescale = jnp.exp(row_top - new_top)
            fresh = jnp.where(allowed, jnp.exp(masked - new_top[..., None]), 0.0)
            return (
                new_top,
                row_mass * rescale + jnp.sum(fresh, axis=-1),
                row_wsum * rescale + jnp.sum(fresh * d_prob, axis=-1),
            )

        start = (
            jnp.full((kv_heads, groups, KEY_BLOCK), -1e30, jnp.float32),
            jnp.zeros((kv_heads, groups, KEY_BLOCK), jnp.float32),
            jnp.zeros((kv_heads, groups, KEY_BLOCK), jnp.float32),
        )
        row_top, row_mass, row_wsum = lax.fori_loop(0, query_block + 1, stats_visit, start)
        first = query_block * KEY_BLOCK
        return (
            lax.dynamic_update_slice_in_dim(top_all, row_top, first, 2),
            lax.dynamic_update_slice_in_dim(mass_all, row_mass, first, 2),
            lax.dynamic_update_slice_in_dim(wsum_all, row_wsum, first, 2),
        )

    start_arrays = (
        jnp.zeros((kv_heads, groups, row_total), jnp.float32),
        jnp.ones((kv_heads, groups, row_total), jnp.float32),
        jnp.zeros((kv_heads, groups, row_total), jnp.float32),
    )
    row_top, row_mass, row_wsum = lax.fori_loop(0, block_count, stats_tile, start_arrays)
    log_norm = row_top + jnp.log(row_mass)
    row_delta = row_wsum / row_mass

    def key_tile_grads(key_block_id, grads):
        grad_q, grad_k, grad_v = grads

        def key_visit(query_block, carry):
            grad_q_now, key_part, value_part = carry
            q_tile, d_tile, key_tile, allowed, scores, d_prob = tile_pair(query_block, key_block_id)
            query_first = query_block * KEY_BLOCK
            norm_tile = lax.dynamic_slice_in_dim(log_norm, query_first, KEY_BLOCK, 2)
            delta_tile = lax.dynamic_slice_in_dim(row_delta, query_first, KEY_BLOCK, 2)
            weights = jnp.where(allowed, jnp.exp(scores - norm_tile[..., None]), 0.0)
            d_score = (weights * (d_prob - delta_tile[..., None])).astype(jnp.bfloat16)
            weights_b = weights.astype(jnp.bfloat16)
            value_part = value_part + jnp.einsum(
                "kgtj,tkgd->jkd", weights_b, d_tile, preferred_element_type=jnp.float32
            )
            key_part = key_part + jnp.einsum(
                "kgtj,tkgd->jkd", d_score, q_tile, preferred_element_type=jnp.float32
            )
            query_part = jnp.einsum(
                "kgtj,jkd->tkgd", d_score, key_tile, preferred_element_type=jnp.float32
            )
            previous = lax.dynamic_slice_in_dim(grad_q_now, query_first, KEY_BLOCK, 0)
            grad_q_now = lax.dynamic_update_slice_in_dim(
                grad_q_now, previous + query_part, query_first, 0
            )
            return (grad_q_now, key_part, value_part)

        start = (
            grad_q,
            jnp.zeros((KEY_BLOCK, kv_heads, HEAD_DIM), jnp.float32),
            jnp.zeros((KEY_BLOCK, kv_heads, HEAD_DIM), jnp.float32),
        )
        grad_q, key_part, value_part = lax.fori_loop(key_block_id, block_count, key_visit, start)
        key_first = key_block_id * KEY_BLOCK
        grad_k = lax.dynamic_update_slice_in_dim(grad_k, key_part * score_scale, key_first, 0)
        grad_v = lax.dynamic_update_slice_in_dim(grad_v, value_part, key_first, 0)
        return (grad_q, grad_k, grad_v)

    start_grads = (
        jnp.zeros((row_total, kv_heads, groups, HEAD_DIM), jnp.float32),
        jnp.zeros((row_total, kv_heads, HEAD_DIM), jnp.float32),
        jnp.zeros((row_total, kv_heads, HEAD_DIM), jnp.float32),
    )
    grad_q, grad_k, grad_v = lax.fori_loop(0, block_count, key_tile_grads, start_grads)
    return (
        (grad_q * score_scale).reshape(row_total, columns),
        grad_k.reshape(row_total, kv_heads * HEAD_DIM),
        grad_v.reshape(row_total, kv_heads * HEAD_DIM),
    )


def local(
    query_heads,
    key_heads,
    value_heads,
    logp_grad,
    logp_new,
    logp_old,
    advantage,
    ratio_caps,
    live_counts,
    seq_begin,
    seg_begin,
    policy_version,
):
    row_total = query_heads.shape[0]
    window = min(max(row_total // 4, KEY_BLOCK), row_total)
    positions = jnp.arange(row_total, dtype=jnp.int32)
    new_logp, old_logp, advantages = (
        lax.all_gather(logp_new, "tensor", axis=0, tiled=True),
        lax.all_gather(logp_old, "tensor", axis=0, tiled=True),
        lax.all_gather(advantage, "tensor", axis=0, tiled=True),
    )
    all_counts = lax.all_gather(live_counts, "dp", axis=0, tiled=True)
    devices = lax.axis_size("dp")
    own_count = live_counts[0]
    live_total = jnp.sum(all_counts.astype(jnp.float32))
    same_seg = (seg_begin[:, None] == seg_begin[None, :]).astype(jnp.float32)
    seg_sum = jnp.dot(same_seg, new_logp - old_logp, precision=lax.Precision.HIGHEST)
    seg_len = jnp.sum(same_seg, axis=1)
    version_ids = jnp.arange(ratio_caps.shape[0], dtype=jnp.int32)
    row_caps = jnp.sum(
        jnp.where(policy_version[:, None] == version_ids[None, :], ratio_caps[None, :], 0.0), axis=1
    )
    weight = jnp.minimum(jnp.exp(seg_sum / seg_len), row_caps)
    loss_coef = jnp.where(
        positions < own_count, -advantages * weight * (row_total * devices / live_total), 0.0
    )
    d_out = (loss_coef[:, None] * logp_grad.astype(jnp.float32)).astype(jnp.bfloat16)
    device = lax.axis_index("dp")
    partner = devices - 1 - device
    target = jnp.clip((own_count - all_counts[partner]) // 2, 0, window)
    begins = (seq_begin == positions) & (positions >= own_count - target) & (positions < own_count)
    boundary = jnp.min(jnp.where(begins, positions, own_count))
    kept_grad = jnp.where((positions < boundary)[:, None], d_out, jnp.zeros_like(d_out))
    own_grads = attend_grad(
        query_heads,
        key_heads,
        value_heads,
        kept_grad,
        seq_begin,
        positions,
        (boundary + KEY_BLOCK - 1) // KEY_BLOCK,
    )

    def window_of(source):
        padded = jnp.concatenate(
            [source, jnp.zeros((window,) + source.shape[1:], source.dtype)], axis=0
        )
        return lax.dynamic_slice_in_dim(padded, boundary, window, 0)

    offsets = seq_begin - positions
    parcel = (
        window_of(query_heads),
        window_of(key_heads),
        window_of(value_heads),
        window_of(d_out),
        window_of(offsets),
        (own_count - boundary)[None],
    )
    for bit_index in range(devices.bit_length() - 1):
        parcel = swapped(
            (parcel[0], parcel[1], parcel[2], parcel[3], for_sending(parcel[4]), parcel[5]),
            "dp",
            bit_index,
        )
    guest_q, guest_k, guest_v, guest_dout, guest_offsets, guest_moved = parcel
    slot_rows = jnp.arange(window, dtype=jnp.int32)
    guest_grads = attend_grad(
        guest_q,
        guest_k,
        guest_v,
        guest_dout,
        slot_rows + guest_offsets,
        slot_rows,
        (guest_moved[0] + KEY_BLOCK - 1) // KEY_BLOCK,
    )
    returned = tuple((member.astype(jnp.bfloat16) for member in guest_grads))
    for bit_index in range(devices.bit_length() - 1):
        returned = jax.tree.map(
            lambda part, own: part.astype(own.dtype),
            swapped(for_sending(returned), "dp", bit_index),
            returned,
        )
    combined = []
    for own_grad, guest_grad in zip(own_grads, returned):
        holder = jnp.zeros((row_total + window, own_grad.shape[1]), jnp.float32)
        placed = lax.dynamic_update_slice_in_dim(
            holder, guest_grad.astype(jnp.float32), boundary, 0
        )[:row_total]
        combined.append(own_grad + placed)
    results = tuple(combined)
    return (
        results[0].astype(jnp.bfloat16),
        results[1].astype(jnp.bfloat16),
        results[2].astype(jnp.bfloat16),
    )


def solution(mesh):
    return jax.shard_map(
        local,
        mesh=mesh,
        in_specs=(
            P("dp", "tensor"),
            P("dp", "tensor"),
            P("dp", "tensor"),
            P("dp", "tensor"),
            P(("dp", "tensor")),
            P(("dp", "tensor")),
            P(("dp", "tensor")),
            P(),
            P("dp"),
            P("dp"),
            P("dp"),
            P("dp"),
        ),
        out_specs=(P("dp", "tensor"), P("dp", "tensor"), P("dp", "tensor")),
        check_vma=False,
    )
```

profile of v0, /device:TPU:70, one launch (start us, length us, event | category | flops | bytes accessed | tf_op | source)
XLA Modules:
  0.0 438.1 jit_solution(10536956630413403971)
XLA Ops:
  3.5 20.5 %all-reduce.5 = s32[64]{0:T(128)S(1)} all-reduce(s32[64]{0:T(128)S(1)} %dynamic-update-slice), channel_id=1, replica_groups=mesh['dp'=64,'tensor'=8] {'dp'}, use_global_device_ids=true, to_apply=%add.5 | all-reduce | flops 64 | bytes 512
  36.3 44.1 %all-reduce.9 = (f32[512]{0:T(512)S(1)}, f32[512]{0:T(512)S(1)}, f32[512]{0:T(512)S(1)}) all-reduce(f32[512]{0:T(512)S(1)} %dynamic-update-slice.1, f32[512]{0:T(512)S(1)} %dynamic-update-slice.2, f32[512]{0:T(512)S(1)} %dynamic-update-slice.3), channel_id=1, replica_groups=mesh['dp'=64,'tensor'=8] {'tensor'}, use_global_device_ids=true, to_apply=%add.6 | all-reduce | flops 1536 | bytes 12288
  91.7 5.3 %collective-permute-done.19 = bf16[128,1024]{0,1:T(8,128)(2,1)S(1)} collective-permute-done((bf16[128,1024]{0,1:T(8,128)(2,1)}, bf16[128,1024]{0,1:T(8,128)(2,1)S(1)}, u32[]{:S(2)}, u32[]{:S(2)}) %collective-permute-start.19) | collective-permute-done | bytes 262176 | tf_op jit(solution)/shard_map/ppermute | solution.py:15
  102.7 4.4 %collective-permute-start.32 = (bf16[128,1024]{0,1:T(8,128)(2,1)S(1)}, bf16[128,1024]{0,1:T(8,128)(2,1)S(1)}, u32[]{:S(2)}, u32[]{:S(2)}) collective-permute-start(bf16[128,1024]{0,1:T(8,128)(2,1)S(1)} %collective-permute-done.31), channel_id=1, source_target_pairs={{0,32},{8,40},{16,48},{24,56},{32,0},{40,8},{48,16},{56,24},{64,96... | collective-permute-start | bytes 786440 | tf_op jit(solution)/shard_map/ppermute | solution.py:15
  107.1 11.0 %collective-permute-done.20 = bf16[128,1024]{0,1:T(8,128)(2,1)S(1)} collective-permute-done((bf16[128,1024]{0,1:T(8,128)(2,1)S(1)}, bf16[128,1024]{0,1:T(8,128)(2,1)S(1)}, u32[]{:S(2)}, u32[]{:S(2)}) %collective-permute-start.20) | collective-permute-done | bytes 262176 | tf_op jit(solution)/shard_map/ppermute | solution.py:15
  118.1 5.4 %collective-permute-start.21 = (bf16[128,1024]{0,1:T(8,128)(2,1)S(1)}, bf16[128,1024]{0,1:T(8,128)(2,1)S(1)}, u32[]{:S(2)}, u32[]{:S(2)}) collective-permute-start(bf16[128,1024]{0,1:T(8,128)(2,1)S(1)} %collective-permute-done.20), channel_id=1, source_target_pairs={{0,64},{8,72},{16,80},{24,88},{32,96},{40,104},{48,112},{56,120},{... | collective-permute-start | bytes 786440 | tf_op jit(solution)/shard_map/ppermute | solution.py:15
  123.5 13.9 %collective-permute-start.33 = (bf16[128,1024]{0,1:T(8,128)(2,1)S(1)}, bf16[128,1024]{0,1:T(8,128)(2,1)S(1)}, u32[]{:S(2)}, u32[]{:S(2)}) collective-permute-start(bf16[128,1024]{0,1:T(8,128)(2,1)S(1)} %collective-permute-done.32), channel_id=1, source_target_pairs={{0,64},{8,72},{16,80},{24,88},{32,96},{40,104},{48,112},{56,120},{... | collective-permute-start | bytes 786440 | tf_op jit(solution)/shard_map/ppermute | solution.py:15
  137.5 13.5 %collective-permute-done.21 = bf16[128,1024]{0,1:T(8,128)(2,1)S(1)} collective-permute-done((bf16[128,1024]{0,1:T(8,128)(2,1)S(1)}, bf16[128,1024]{0,1:T(8,128)(2,1)S(1)}, u32[]{:S(2)}, u32[]{:S(2)}) %collective-permute-start.21) | collective-permute-done | bytes 262176 | tf_op jit(solution)/shard_map/ppermute | solution.py:15
  164.5 13.8 %collective-permute-start.13 = (bf16[128,128]{1,0:T(8,128)(2,1)S(1)}, bf16[128,128]{1,0:T(8,128)(2,1)S(1)}, u32[]{:S(2)}, u32[]{:S(2)}) collective-permute-start(bf16[128,128]{1,0:T(8,128)(2,1)S(1)} %collective-permute-done.12), channel_id=1, source_target_pairs={{0,16},{8,24},{16,0},{24,8},{32,48},{40,56},{48,32},{56,40},{64,80... | collective-permute-start | bytes 98312 | tf_op jit(solution)/shard_map/ppermute | solution.py:15
  180.2 7.7 %collective-permute-start.14 = (bf16[128,128]{1,0:T(8,128)(2,1)S(1)}, bf16[128,128]{1,0:T(8,128)(2,1)S(1)}, u32[]{:S(2)}, u32[]{:S(2)}) collective-permute-start(bf16[128,128]{1,0:T(8,128)(2,1)S(1)} %collective-permute-done.13), channel_id=1, source_target_pairs={{0,32},{8,40},{16,48},{24,56},{32,0},{40,8},{48,16},{56,24},{64,96... | collective-permute-start | bytes 98312 | tf_op jit(solution)/shard_map/ppermute | solution.py:15
  189.9 5.4 %collective-permute-start.15 = (bf16[128,128]{1,0:T(8,128)(2,1)S(1)}, bf16[128,128]{1,0:T(8,128)(2,1)S(1)}, u32[]{:S(2)}, u32[]{:S(2)}) collective-permute-start(bf16[128,128]{1,0:T(8,128)(2,1)S(1)} %collective-permute-done.14), channel_id=1, source_target_pairs={{0,64},{8,72},{16,80},{24,88},{32,96},{40,104},{48,112},{56,120},{... | collective-permute-start | bytes 98312 | tf_op jit(solution)/shard_map/ppermute | solution.py:15
  195.3 4.3 collective-permute-start.27
  208.9 5.2 %collective-permute-start.23 = (bf16[128,1024]{0,1:T(8,128)(2,1)S(1)}, bf16[128,1024]{0,1:T(8,128)(2,1)S(1)}, u32[]{:S(2)}, u32[]{:S(2)}) collective-permute-start(bf16[128,1024]{0,1:T(8,128)(2,1)S(1)} %collective-permute-done.22), channel_id=1, source_target_pairs={{0,256},{8,264},{16,272},{24,280},{32,288},{40,296},{48,304},{56,3... | collective-permute-start | bytes 786440 | tf_op jit(solution)/shard_map/ppermute | solution.py:15
  221.8 4.8 %collective-permute-start.2 = (s32[1]{0:T(128)}, s32[1]{0:T(128)}, u32[]{:S(2)}, u32[]{:S(2)}) collective-permute-start(s32[1]{0:T(128)} %collective-permute-done.1), channel_id=1, source_target_pairs={{0,32},{8,40},{16,48},{24,56},{32,0},{40,8},{48,16},{56,24},{64,96... | collective-permute-start | bytes 20 | tf_op jit(solution)/shard_map/ppermute | solution.py:15
  228.1 5.4 %collective-permute-start.3 = (s32[1]{0:T(128)}, s32[1]{0:T(128)}, u32[]{:S(2)}, u32[]{:S(2)}) collective-permute-start(s32[1]{0:T(128)} %collective-permute-done.2), channel_id=1, source_target_pairs={{0,64},{8,72},{16,80},{24,88},{32,96},{40,104},{48,112},{56,120},{... | collective-permute-start | bytes 20 | tf_op jit(solution)/shard_map/ppermute | solution.py:15
  242.9 5.2 %collective-permute-start.5 = (s32[1]{0:T(128)}, s32[1]{0:T(128)}, u32[]{:S(2)}, u32[]{:S(2)}) collective-permute-start(s32[1]{0:T(128)} %collective-permute-done.4), channel_id=1, source_target_pairs={{0,256},{8,264},{16,272},{24,280},{32,288},{40,296},{48,304},{56,3... | collective-permute-start | bytes 20 | tf_op jit(solution)/shard_map/ppermute | solution.py:15
  258.3 4.8 %collective-permute-start.8 = (s32[128]{0:T(128)S(1)}, s32[128]{0:T(128)S(1)}, u32[]{:S(2)}, u32[]{:S(2)}) collective-permute-start(s32[128]{0:T(128)S(1)} %collective-permute-done.7), channel_id=1, source_target_pairs={{0,32},{8,40},{16,48},{24,56},{32,0},{40,8},{48,16},{56,24},{64,96... | collective-permute-start | bytes 1544 | tf_op jit(solution)/shard_map/ppermute | solution.py:15
  264.6 5.4 %collective-permute-start.9 = (s32[128]{0:T(128)S(1)}, s32[128]{0:T(128)S(1)}, u32[]{:S(2)}, u32[]{:S(2)}) collective-permute-start(s32[128]{0:T(128)S(1)} %collective-permute-done.8), channel_id=1, source_target_pairs={{0,64},{8,72},{16,80},{24,88},{32,96},{40,104},{48,112},{56,120},{... | collective-permute-start | bytes 1544 | tf_op jit(solution)/shard_map/ppermute | solution.py:15
  279.3 5.2 %collective-permute-start.11 = (s32[128]{0:T(128)S(1)}, s32[128]{0:T(128)S(1)}, u32[]{:S(2)}, u32[]{:S(2)}) collective-permute-start(s32[128]{0:T(128)S(1)} %collective-permute-done.10), channel_id=1, source_target_pairs={{0,256},{8,264},{16,272},{24,280},{32,288},{40,296},{48,304},{56,3... | collective-permute-start | bytes 1544 | tf_op jit(solution)/shard_map/ppermute | solution.py:15
  286.7 5.2 %collective-permute-start.29 = (bf16[128,128]{1,0:T(8,128)(2,1)S(1)}, bf16[128,128]{1,0:T(8,128)(2,1)S(1)}, u32[]{:S(2)}, u32[]{:S(2)}) collective-permute-start(bf16[128,128]{1,0:T(8,128)(2,1)S(1)} %collective-permute-done.28), channel_id=1, source_target_pairs={{0,256},{8,264},{16,272},{24,280},{32,288},{40,296},{48,304},{56,3... | collective-permute-start | bytes 98312 | tf_op jit(solution)/shard_map/ppermute | solution.py:15
  323.5 4.8 %collective-permute-start.38 = (bf16[128,1024]{1,0:T(8,128)(2,1)}, bf16[128,1024]{1,0:T(8,128)(2,1)}, u32[]{:S(2)}, u32[]{:S(2)}) collective-permute-start(bf16[128,1024]{1,0:T(8,128)(2,1)} %collective-permute-done.37), channel_id=1, source_target_pairs={{0,32},{8,40},{16,48},{24,56},{32,0},{40,8},{48,16},{56,24},{64,96... | collective-permute-start | bytes 786440 | tf_op jit(solution)/shard_map/ppermute | solution.py:15
  328.4 16.7 %while.128 = (s32[]{:T(128)}, f32[1,8,512]{2,1,0:T(8,128)S(1)}, f32[1,8,512]{2,1,0:T(8,128)S(1)}, f32[1,8,512]{2,1,0:T(8,128)S(1)}, s32[]{:T(128)}, /*index=5*/s...) while((s32[]{:T(128)}, f32[1,8,512]{2,1,0:T(8,128)S(1)}, ...), condition=%wide.region_10.11_spmd, body=%wide.region_4.10_spmd.sunk | while | flops 68471944 | bytes 3392094 | solution.py:84
  333.9 4.6 %while.135 = (s32[]{:T(128)}, f32[1,8,128]{2,1,0:T(8,128)S(1)}, f32[1,8,128]{2,1,0:T(8,128)S(1)}, f32[1,8,128]{2,1,0:T(8,128)S(1)}, s32[]{:T(128)}, /*index=5*/s...) while((s32[]{:T(128)}, f32[1,8,128]{2,1,0:T(8,128)S(1)}, ...), condition=%wide.region_9.9_spmd, body=%wide.region_5.8_spmd.sunk | while | flops 68471936 | bytes 2304199 | solution.py:71
  338.8 6.2 %while.135 = (s32[]{:T(128)}, f32[1,8,128]{2,1,0:T(8,128)S(1)}, f32[1,8,128]{2,1,0:T(8,128)S(1)}, f32[1,8,128]{2,1,0:T(8,128)S(1)}, s32[]{:T(128)}, /*index=5*/s...) while((s32[]{:T(128)}, f32[1,8,128]{2,1,0:T(8,128)S(1)}, ...), condition=%wide.region_9.9_spmd, body=%wide.region_5.8_spmd.sunk | while | flops 68471936 | bytes 2304199 | solution.py:71
  351.8 5.0 %collective-permute-start.51 = (bf16[128,128]{1,0:T(8,128)(2,1)S(1)}, bf16[128,128]{1,0:T(8,128)(2,1)}, u32[]{:S(2)}, u32[]{:S(2)}) collective-permute-start(bf16[128,128]{1,0:T(8,128)(2,1)S(1)} %collective-permute-done.50), channel_id=1, source_target_pairs={{0,64},{8,72},{16,80},{24,88},{32,96},{40,104},{48,112},{56,120},{... | collective-permute-start | bytes 98312 | tf_op jit(solution)/shard_map/ppermute | solution.py:15
  359.1 4.4 %collective-permute-start.39 = (bf16[128,1024]{1,0:T(8,128)(2,1)}, bf16[128,1024]{1,0:T(8,128)(2,1)}, u32[]{:S(2)}, u32[]{:S(2)}) collective-permute-start(bf16[128,1024]{1,0:T(8,128)(2,1)} %collective-permute-done.38), channel_id=1, source_target_pairs={{0,64},{8,72},{16,80},{24,88},{32,96},{40,104},{48,112},{56,120},{... | collective-permute-start | bytes 786440 | tf_op jit(solution)/shard_map/ppermute | solution.py:15
  365.1 42.2 %while.130 = (s32[]{:T(128)}, f32[512,1,8,128]{3,0,2,1:T(8,128)S(1)}, f32[512,1,128]{2,0,1:T(8,128)}, f32[512,1,128]{2,0,1:T(8,128)}, s32[]{:T(128)}, /*index=5*...) while((s32[]{:T(128)}, ...), condition=%wide.region_14.15_spmd.clone, body=%wide.region_11.14_spmd.clone.sunk | while | flops 168919168 | bytes 5798542 | solution.py:131
  366.1 14.1 %while.136 = (s32[]{:T(128)}, f32[512,1,8,128]{3,0,2,1:T(8,128)S(1)}, f32[128,1,128]{0,2,1:T(8,128)S(1)}, f32[128,1,128]{0,2,1:T(8,128)S(1)}, s32[]{:T(128)}, /*...) while((s32[]{:T(128)}, ...), condition=%wide.region_13.13_spmd, body=%wide.region_12.12_spmd.sunk | while | flops 168902784 | bytes 4878583 | solution.py:120
  381.9 10.6 %while.136 = (s32[]{:T(128)}, f32[512,1,8,128]{3,0,2,1:T(8,128)S(1)}, f32[128,1,128]{0,2,1:T(8,128)S(1)}, f32[128,1,128]{0,2,1:T(8,128)S(1)}, s32[]{:T(128)}, /*...) while((s32[]{:T(128)}, ...), condition=%wide.region_13.13_spmd, body=%wide.region_12.12_spmd.sunk | while | flops 168902784 | bytes 4878583 | solution.py:120
  394.1 7.1 %while.136 = (s32[]{:T(128)}, f32[512,1,8,128]{3,0,2,1:T(8,128)S(1)}, f32[128,1,128]{0,2,1:T(8,128)S(1)}, f32[128,1,128]{0,2,1:T(8,128)S(1)}, s32[]{:T(128)}, /*...) while((s32[]{:T(128)}, ...), condition=%wide.region_13.13_spmd, body=%wide.region_12.12_spmd.sunk | while | flops 168902784 | bytes 4878583 | solution.py:120
  417.8 6.0 %collective-permute-start.53 = (bf16[128,128]{1,0:T(8,128)(2,1)}, bf16[128,128]{1,0:T(8,128)(2,1)S(1)}, u32[]{:S(2)}, u32[]{:S(2)}) collective-permute-start(bf16[128,128]{1,0:T(8,128)(2,1)} %collective-permute-done.52), channel_id=1, source_target_pairs={{0,256},{8,264},{16,272},{24,280},{32,288},{40,296},{48,304},{56,3... | collective-permute-start | bytes 98312 | tf_op jit(solution)/shard_map/ppermute | solution.py:15
  428.4 5.8 %collective-permute-done.41 = bf16[128,1024]{1,0:T(8,128)(2,1)S(1)} collective-permute-done((bf16[128,1024]{1,0:T(8,128)(2,1)S(1)}, bf16[128,1024]{1,0:T(8,128)(2,1)S(1)}, u32[]{:S(2)}, u32[]{:S(2)}) %collective-permute-start.41) | collective-permute-done | bytes 262176 | tf_op jit(solution)/shard_map/ppermute | solution.py:15
  (469 shorter events, 223.7 us)
Async XLA Ops:
  30.2 55.6 %collective-permute-start.18 = (bf16[128,1024]{0,1:T(8,128)(2,1)S(1)}, bf16[128,1024]{0,1:T(8,128)(2,1)}, u32[]{:S(2)}, u32[]{:S(2)}) collective-permute-start(bf16[128,1024]{0,1:T(8,128)(2,1)S(1)} %pad_dynamic-slice_fusion.1), channel_id=1, source_target_pairs={{0,8},{8,0},{16,24},{24,16},{32,40},{40,32},{48,56},{56,48},{64,72... | collective-permute-start | bytes 786440 | tf_op jit(solution)/shard_map/ppermute | solution.py:15
  85.8 11.2 %collective-permute-start.19 = (bf16[128,1024]{0,1:T(8,128)(2,1)}, bf16[128,1024]{0,1:T(8,128)(2,1)S(1)}, u32[]{:S(2)}, u32[]{:S(2)}) collective-permute-start(bf16[128,1024]{0,1:T(8,128)(2,1)} %collective-permute-done.18), channel_id=1, source_target_pairs={{0,16},{8,24},{16,0},{24,8},{32,48},{40,56},{48,32},{56,40},{64,80... | collective-permute-start | bytes 786440 | tf_op jit(solution)/shard_map/ppermute | solution.py:15
  88.8 13.9 %collective-permute-start.31 = (bf16[128,1024]{0,1:T(8,128)(2,1)S(1)}, bf16[128,1024]{0,1:T(8,128)(2,1)S(1)}, u32[]{:S(2)}, u32[]{:S(2)}) collective-permute-start(bf16[128,1024]{0,1:T(8,128)(2,1)S(1)} %collective-permute-done.30), channel_id=1, source_target_pairs={{0,16},{8,24},{16,0},{24,8},{32,48},{40,56},{48,32},{56,40},{64,80... | collective-permute-start | bytes 786440 | tf_op jit(solution)/shard_map/ppermute | solution.py:15
  97.0 21.0 %collective-permute-start.20 = (bf16[128,1024]{0,1:T(8,128)(2,1)S(1)}, bf16[128,1024]{0,1:T(8,128)(2,1)S(1)}, u32[]{:S(2)}, u32[]{:S(2)}) collective-permute-start(bf16[128,1024]{0,1:T(8,128)(2,1)S(1)} %collective-permute-done.19), channel_id=1, source_target_pairs={{0,32},{8,40},{16,48},{24,56},{32,0},{40,8},{48,16},{56,24},{64,96... | collective-permute-start | bytes 786440 | tf_op jit(solution)/shard_map/ppermute | solution.py:15
  102.7 20.9 %collective-permute-start.32 = (bf16[128,1024]{0,1:T(8,128)(2,1)S(1)}, bf16[128,1024]{0,1:T(8,128)(2,1)S(1)}, u32[]{:S(2)}, u32[]{:S(2)}) collective-permute-start(bf16[128,1024]{0,1:T(8,128)(2,1)S(1)} %collective-permute-done.31), channel_id=1, source_target_pairs={{0,32},{8,40},{16,48},{24,56},{32,0},{40,8},{48,16},{56,24},{64,96... | collective-permute-start | bytes 786440 | tf_op jit(solution)/shard_map/ppermute | solution.py:15
  118.1 32.9 %collective-permute-start.21 = (bf16[128,1024]{0,1:T(8,128)(2,1)S(1)}, bf16[128,1024]{0,1:T(8,128)(2,1)S(1)}, u32[]{:S(2)}, u32[]{:S(2)}) collective-permute-start(bf16[128,1024]{0,1:T(8,128)(2,1)S(1)} %collective-permute-done.20), channel_id=1, source_target_pairs={{0,64},{8,72},{16,80},{24,88},{32,96},{40,104},{48,112},{56,120},{... | collective-permute-start | bytes 786440 | tf_op jit(solution)/shard_map/ppermute | solution.py:15
  123.5 32.9 %collective-permute-start.33 = (bf16[128,1024]{0,1:T(8,128)(2,1)S(1)}, bf16[128,1024]{0,1:T(8,128)(2,1)S(1)}, u32[]{:S(2)}, u32[]{:S(2)}) collective-permute-start(bf16[128,1024]{0,1:T(8,128)(2,1)S(1)} %collective-permute-done.32), channel_id=1, source_target_pairs={{0,64},{8,72},{16,80},{24,88},{32,96},{40,104},{48,112},{56,120},{... | collective-permute-start | bytes 786440 | tf_op jit(solution)/shard_map/ppermute | solution.py:15
  151.0 57.9 %collective-permute-start.22 = (bf16[128,1024]{0,1:T(8,128)(2,1)S(1)}, bf16[128,1024]{0,1:T(8,128)(2,1)S(1)}, u32[]{:S(2)}, u32[]{:S(2)}) collective-permute-start(bf16[128,1024]{0,1:T(8,128)(2,1)S(1)} %collective-permute-done.21), channel_id=1, source_target_pairs={{0,128},{8,136},{16,144},{24,152},{32,160},{40,168},{48,176},{56,1... | collective-permute-start | bytes 786440 | tf_op jit(solution)/shard_map/ppermute | solution.py:15
  156.5 57.6 %collective-permute-start.34 = (bf16[128,1024]{0,1:T(8,128)(2,1)S(1)}, bf16[128,1024]{0,1:T(8,128)(2,1)S(1)}, u32[]{:S(2)}, u32[]{:S(2)}) collective-permute-start(bf16[128,1024]{0,1:T(8,128)(2,1)S(1)} %collective-permute-done.33), channel_id=1, source_target_pairs={{0,128},{8,136},{16,144},{24,152},{32,160},{40,168},{48,176},{56,1... | collective-permute-start | bytes 786440 | tf_op jit(solution)/shard_map/ppermute | solution.py:15
  162.1 16.2 %collective-permute-start.24 = (bf16[128,128]{1,0:T(8,128)(2,1)S(1)}, bf16[128,128]{1,0:T(8,128)(2,1)S(1)}, u32[]{:S(2)}, u32[]{:S(2)}) collective-permute-start(bf16[128,128]{1,0:T(8,128)(2,1)S(1)} %pad_dynamic-slice_fusion.2), channel_id=1, source_target_pairs={{0,8},{8,0},{16,24},{24,16},{32,40},{40,32},{48,56},{56,48},{64,72... | collective-permute-start | bytes 98312 | tf_op jit(solution)/shard_map/ppermute | solution.py:15
  164.5 15.7 %collective-permute-start.13 = (bf16[128,128]{1,0:T(8,128)(2,1)S(1)}, bf16[128,128]{1,0:T(8,128)(2,1)S(1)}, u32[]{:S(2)}, u32[]{:S(2)}) collective-permute-start(bf16[128,128]{1,0:T(8,128)(2,1)S(1)} %collective-permute-done.12), channel_id=1, source_target_pairs={{0,16},{8,24},{16,0},{24,8},{32,48},{40,56},{48,32},{56,40},{64,80... | collective-permute-start | bytes 98312 | tf_op jit(solution)/shard_map/ppermute | solution.py:15
  178.3 9.6 %collective-permute-start.25 = (bf16[128,128]{1,0:T(8,128)(2,1)S(1)}, bf16[128,128]{1,0:T(8,128)(2,1)S(1)}, u32[]{:S(2)}, u32[]{:S(2)}) collective-permute-start(bf16[128,128]{1,0:T(8,128)(2,1)S(1)} %collective-permute-done.24), channel_id=1, source_target_pairs={{0,16},{8,24},{16,0},{24,8},{32,48},{40,56},{48,32},{56,40},{64,80... | collective-permute-start | bytes 98312 | tf_op jit(solution)/shard_map/ppermute | solution.py:15
  189.9 13.1 %collective-permute-start.15 = (bf16[128,128]{1,0:T(8,128)(2,1)S(1)}, bf16[128,128]{1,0:T(8,128)(2,1)S(1)}, u32[]{:S(2)}, u32[]{:S(2)}) collective-permute-start(bf16[128,128]{1,0:T(8,128)(2,1)S(1)} %collective-permute-done.14), channel_id=1, source_target_pairs={{0,64},{8,72},{16,80},{24,88},{32,96},{40,104},{48,112},{56,120},{... | collective-permute-start | bytes 98312 | tf_op jit(solution)/shard_map/ppermute | solution.py:15
  195.3 10.7 %collective-permute-start.27 = (bf16[128,128]{1,0:T(8,128)(2,1)S(1)}, bf16[128,128]{1,0:T(8,128)(2,1)S(1)}, u32[]{:S(2)}, u32[]{:S(2)}) collective-permute-start(bf16[128,128]{1,0:T(8,128)(2,1)S(1)} %collective-permute-done.26), channel_id=1, source_target_pairs={{0,64},{8,72},{16,80},{24,88},{32,96},{40,104},{48,112},{56,120},{... | collective-permute-start | bytes 98312 | tf_op jit(solution)/shard_map/ppermute | solution.py:15
  200.3 16.1 %collective-permute-start = (s32[1]{0:T(128)}, s32[1]{0:T(128)}, u32[]{:S(2)}, u32[]{:S(2)}) collective-permute-start(s32[1]{0:T(128)} %bitcast.72), channel_id=1, source_target_pairs={{0,8},{8,0},{16,24},{24,16},{32,40},{40,32},{48,56},{56,48},{64,72... | collective-permute-start | bytes 20 | tf_op jit(solution)/shard_map/ppermute | solution.py:15
  203.0 81.6 %collective-permute-start.16 = (bf16[128,128]{1,0:T(8,128)(2,1)S(1)}, bf16[128,128]{1,0:T(8,128)(2,1)S(1)}, u32[]{:S(2)}, u32[]{:S(2)}) collective-permute-start(bf16[128,128]{1,0:T(8,128)(2,1)S(1)} %collective-permute-done.15), channel_id=1, source_target_pairs={{0,128},{8,136},{16,144},{24,152},{32,160},{40,168},{48,176},{56,1... | collective-permute-start | bytes 98312 | tf_op jit(solution)/shard_map/ppermute | solution.py:15
  206.1 80.6 %collective-permute-start.28 = (bf16[128,128]{1,0:T(8,128)(2,1)S(1)}, bf16[128,128]{1,0:T(8,128)(2,1)S(1)}, u32[]{:S(2)}, u32[]{:S(2)}) collective-permute-start(bf16[128,128]{1,0:T(8,128)(2,1)S(1)} %collective-permute-done.27), channel_id=1, source_target_pairs={{0,128},{8,136},{16,144},{24,152},{32,160},{40,168},{48,176},{56,1... | collective-permute-start | bytes 98312 | tf_op jit(solution)/shard_map/ppermute | solution.py:15
  208.9 83.1 %collective-permute-start.23 = (bf16[128,1024]{0,1:T(8,128)(2,1)S(1)}, bf16[128,1024]{0,1:T(8,128)(2,1)S(1)}, u32[]{:S(2)}, u32[]{:S(2)}) collective-permute-start(bf16[128,1024]{0,1:T(8,128)(2,1)S(1)} %collective-permute-done.22), channel_id=1, source_target_pairs={{0,256},{8,264},{16,272},{24,280},{32,288},{40,296},{48,304},{56,3... | collective-permute-start | bytes 786440 | tf_op jit(solution)/shard_map/ppermute | solution.py:15
  214.1 78.0 %collective-permute-start.35 = (bf16[128,1024]{0,1:T(8,128)(2,1)S(1)}, bf16[128,1024]{0,1:T(8,128)(2,1)S(1)}, u32[]{:S(2)}, u32[]{:S(2)}) collective-permute-start(bf16[128,1024]{0,1:T(8,128)(2,1)S(1)} %collective-permute-done.34), channel_id=1, source_target_pairs={{0,256},{8,264},{16,272},{24,280},{32,288},{40,296},{48,304},{56,3... | collective-permute-start | bytes 786440 | tf_op jit(solution)/shard_map/ppermute | solution.py:15
  279.3 12.6 %collective-permute-start.11 = (s32[128]{0:T(128)S(1)}, s32[128]{0:T(128)S(1)}, u32[]{:S(2)}, u32[]{:S(2)}) collective-permute-start(s32[128]{0:T(128)S(1)} %collective-permute-done.10), channel_id=1, source_target_pairs={{0,256},{8,264},{16,272},{24,280},{32,288},{40,296},{48,304},{56,3... | collective-permute-start | bytes 1544 | tf_op jit(solution)/shard_map/ppermute | solution.py:15
  305.7 17.8 %collective-permute-start.37 = (bf16[128,1024]{1,0:T(8,128)(2,1)}, bf16[128,1024]{1,0:T(8,128)(2,1)}, u32[]{:S(2)}, u32[]{:S(2)}) collective-permute-start(bf16[128,1024]{1,0:T(8,128)(2,1)} %collective-permute-done.36), channel_id=1, source_target_pairs={{0,16},{8,24},{16,0},{24,8},{32,48},{40,56},{48,32},{56,40},{64,80... | collective-permute-start | bytes 786440 | tf_op jit(solution)/shard_map/ppermute | solution.py:15
  319.6 25.5 %collective-permute-start.49 = (bf16[128,128]{1,0:T(8,128)(2,1)S(1)}, bf16[128,128]{1,0:T(8,128)(2,1)S(1)}, u32[]{:S(2)}, u32[]{:S(2)}) collective-permute-start(bf16[128,128]{1,0:T(8,128)(2,1)S(1)} %collective-permute-done.48), channel_id=1, source_target_pairs={{0,16},{8,24},{16,0},{24,8},{32,48},{40,56},{48,32},{56,40},{64,80... | collective-permute-start | bytes 98312 | tf_op jit(solution)/shard_map/ppermute | solution.py:15
  321.5 25.5 %collective-permute-start.44 = (bf16[128,128]{1,0:T(8,128)(2,1)S(1)}, bf16[128,128]{1,0:T(8,128)(2,1)S(1)}, u32[]{:S(2)}, u32[]{:S(2)}) collective-permute-start(bf16[128,128]{1,0:T(8,128)(2,1)S(1)} %collective-permute-done.43), channel_id=1, source_target_pairs={{0,32},{8,40},{16,48},{24,56},{32,0},{40,8},{48,16},{56,24},{64,96... | collective-permute-start | bytes 98312 | tf_op jit(solution)/shard_map/ppermute | solution.py:15
  323.5 35.6 %collective-permute-start.38 = (bf16[128,1024]{1,0:T(8,128)(2,1)}, bf16[128,1024]{1,0:T(8,128)(2,1)}, u32[]{:S(2)}, u32[]{:S(2)}) collective-permute-start(bf16[128,1024]{1,0:T(8,128)(2,1)} %collective-permute-done.37), channel_id=1, source_target_pairs={{0,32},{8,40},{16,48},{24,56},{32,0},{40,8},{48,16},{56,24},{64,96... | collective-permute-start | bytes 786440 | tf_op jit(solution)/shard_map/ppermute | solution.py:15
  347.0 10.1 %collective-permute-start.45 = (bf16[128,128]{1,0:T(8,128)(2,1)S(1)}, bf16[128,128]{1,0:T(8,128)(2,1)}, u32[]{:S(2)}, u32[]{:S(2)}) collective-permute-start(bf16[128,128]{1,0:T(8,128)(2,1)S(1)} %collective-permute-done.44), channel_id=1, source_target_pairs={{0,64},{8,72},{16,80},{24,88},{32,96},{40,104},{48,112},{56,120},{... | collective-permute-start | bytes 98312 | tf_op jit(solution)/shard_map/ppermute | solution.py:15
  351.8 55.5 %collective-permute-start.51 = (bf16[128,128]{1,0:T(8,128)(2,1)S(1)}, bf16[128,128]{1,0:T(8,128)(2,1)}, u32[]{:S(2)}, u32[]{:S(2)}) collective-permute-start(bf16[128,128]{1,0:T(8,128)(2,1)S(1)} %collective-permute-done.50), channel_id=1, source_target_pairs={{0,64},{8,72},{16,80},{24,88},{32,96},{40,104},{48,112},{56,120},{... | collective-permute-start | bytes 98312 | tf_op jit(solution)/shard_map/ppermute | solution.py:15
  357.1 52.1 %collective-permute-start.46 = (bf16[128,128]{1,0:T(8,128)(2,1)}, bf16[128,128]{1,0:T(8,128)(2,1)}, u32[]{:S(2)}, u32[]{:S(2)}) collective-permute-start(bf16[128,128]{1,0:T(8,128)(2,1)} %collective-permute-done.45), channel_id=1, source_target_pairs={{0,128},{8,136},{16,144},{24,152},{32,160},{40,168},{48,176},{56,1... | collective-permute-start | bytes 98312 | tf_op jit(solution)/shard_map/ppermute | solution.py:15
  359.1 52.1 %collective-permute-start.39 = (bf16[128,1024]{1,0:T(8,128)(2,1)}, bf16[128,1024]{1,0:T(8,128)(2,1)}, u32[]{:S(2)}, u32[]{:S(2)}) collective-permute-start(bf16[128,1024]{1,0:T(8,128)(2,1)} %collective-permute-done.38), channel_id=1, source_target_pairs={{0,64},{8,72},{16,80},{24,88},{32,96},{40,104},{48,112},{56,120},{... | collective-permute-start | bytes 786440 | tf_op jit(solution)/shard_map/ppermute | solution.py:15
  407.3 10.6 %collective-permute-start.52 = (bf16[128,128]{1,0:T(8,128)(2,1)}, bf16[128,128]{1,0:T(8,128)(2,1)}, u32[]{:S(2)}, u32[]{:S(2)}) collective-permute-start(bf16[128,128]{1,0:T(8,128)(2,1)} %collective-permute-done.51), channel_id=1, source_target_pairs={{0,128},{8,136},{16,144},{24,152},{32,160},{40,168},{48,176},{56,1... | collective-permute-start | bytes 98312 | tf_op jit(solution)/shard_map/ppermute | solution.py:15
  409.2 14.7 %collective-permute-start.47 = (bf16[128,128]{1,0:T(8,128)(2,1)}, bf16[128,128]{1,0:T(8,128)(2,1)S(1)}, u32[]{:S(2)}, u32[]{:S(2)}) collective-permute-start(bf16[128,128]{1,0:T(8,128)(2,1)} %collective-permute-done.46), channel_id=1, source_target_pairs={{0,256},{8,264},{16,272},{24,280},{32,288},{40,296},{48,304},{56,3... | collective-permute-start | bytes 98312 | tf_op jit(solution)/shard_map/ppermute | solution.py:15
  411.1 13.4 %collective-permute-start.40 = (bf16[128,1024]{1,0:T(8,128)(2,1)}, bf16[128,1024]{1,0:T(8,128)(2,1)S(1)}, u32[]{:S(2)}, u32[]{:S(2)}) collective-permute-start(bf16[128,1024]{1,0:T(8,128)(2,1)} %collective-permute-done.39), channel_id=1, source_target_pairs={{0,128},{8,136},{16,144},{24,152},{32,160},{40,168},{48,176},{56,1... | collective-permute-start | bytes 786440 | tf_op jit(solution)/shard_map/ppermute | solution.py:15
  424.5 9.8 %collective-permute-start.41 = (bf16[128,1024]{1,0:T(8,128)(2,1)S(1)}, bf16[128,1024]{1,0:T(8,128)(2,1)S(1)}, u32[]{:S(2)}, u32[]{:S(2)}) collective-permute-start(bf16[128,1024]{1,0:T(8,128)(2,1)S(1)} %collective-permute-done.40), channel_id=1, source_target_pairs={{0,256},{8,264},{16,272},{24,280},{32,288},{40,296},{48,304},{56,3... | collective-permute-start | bytes 786440 | tf_op jit(solution)/shard_map/ppermute | solution.py:15
  (39 other events, 621.2 us)
where the time goes:
time: 442 us; the launch traced here: 438 us
  starting transfers between devices  203 us (46%)
  waiting for transfers between devices  68 us (15%)
  blocking collectives  64.7 us (15%)
  matrix products  46.9 us (11%)
  local copies, waits for them, and re-layouts  28.7 us (6%)
  other arithmetic  15.7 us (4%)
  between operations  8.31 us (2%)
    ppermute x54, starting transfers between devices, swapped(): lax.ppermute(array, axis, [(i, i ^ 1 << bit) for i in range(lax.axis_size...  203 us
    ppermute x54, waiting for transfers between devices, swapped(): lax.ppermute(array, axis, [(i, i ^ 1 << bit) for i in range(lax.axis_size...  68 us
    unnamed x2, blocking collectives  64.7 us
    dot_general x22, matrix products, tile_pair(): jnp.einsum('tkgd,jkd->kgtj', q_tile, key_tile, preferred_element_type=jnp...  15.2 us
    dot_general x22, matrix products, tile_pair(): jnp.einsum('tkgd,jkd->kgtj', d_tile, value_tile, preferred_element_type=j...  13 us
    dot_general x11, matrix products, key_visit(): jnp.einsum('kgtj,tkgd->jkd', d_score, q_tile, preferred_element_type=jnp....  12.6 us
  transfers between devices with their start and end apart: 54, of which 20 were waited for; matrix products, arithmetic and copies ran while one was open for 17% of the time, Pallas kernels for 0%

commit v1 on v0

v1 whole, which is shorter than its diff:
```python
import functools
import math

import jax
import jax.numpy as jnp
from jax import lax
from jax.experimental import pallas as pl
from jax.experimental.pallas import tpu as pltpu
from jax.sharding import PartitionSpec as P

HEAD_DIM = 128
TILE = 128
MESH = pl.DeviceIdType.MESH
NEG = -1e30


def in_hbm(*arrays):
    return [pltpu.with_memory_space_constraint(a, pltpu.HBM) for a in arrays]


def flips(index, bits):
    return [(1 << b) * (1 - 2 * lax.rem(lax.div(index, 1 << b), 2)) for b in bits]


def partners(index, bits):
    deltas = flips(index, bits)
    found = []
    for mask in range(1, 1 << len(bits)):
        other = index
        for n, delta in enumerate(deltas):
            if mask >> n & 1:
                other = other + delta
        found.append(other)
    return found


def exchange_kernel(plane_bits, line_bits, nt, new_hbm, old_hbm, adv_hbm, cnt_s, gath_ref, total_ref,
                    new_v, old_v, adv_v, own_row, rows, cnt_row, cnt_rows, part_row, part_rows,
                    load_sem, send_sem, recv_sem):
    dp = lax.axis_index("dp")
    me = lax.axis_index("tensor")
    owners = partners(me, range(nt.bit_length() - 1))
    tensor_peers = [(dp, t) for t in owners]
    plane_peers = [(d, me) for d in partners(dp, plane_bits)]
    line_peers = [(d, me) for d in partners(dp, line_bits)]
    planes, nz = len(plane_peers) + 1, len(line_peers) + 1
    peers = tensor_peers + plane_peers + line_peers

    barrier = pltpu.get_barrier_semaphore()
    for peer in peers:
        pl.semaphore_signal(barrier, inc=1, device_id=peer, device_id_type=MESH)
    loads = [
        pltpu.make_async_copy(src, dst, load_sem.at[n])
        for n, (src, dst) in enumerate(
            ((new_hbm, new_v), (old_hbm, old_v), (adv_hbm, adv_v)))
    ]
    for load in loads:
        load.start()
    for load in loads:
        load.wait()
    own_row[0] = jnp.concatenate([new_v[...] - old_v[...], adv_v[...]], axis=1)
    cnt_row[0] = jnp.full((1, 128), cnt_s[0].astype(jnp.float32), jnp.float32)
    pl.semaphore_wait(barrier, len(peers))

    def send(src, dst, n, peer):
        pltpu.make_async_remote_copy(
            src_ref=src, dst_ref=dst, send_sem=send_sem.at[n], recv_sem=recv_sem.at[n],
            device_id=peer, device_id_type=MESH).start()

    def drain(buffer, n, sem):
        span = buffer.at[pl.ds(0, n)]
        pltpu.make_async_copy(span, span, sem).wait()

    for step in range(1, planes):
        send(cnt_row, cnt_rows.at[pl.ds(step - 1, 1)], 0, plane_peers[step - 1])
    for step in range(1, nt):
        send(own_row, rows.at[pl.ds(step - 1, 1)], 1, tensor_peers[step - 1])
    drain(cnt_rows, planes - 1, recv_sem.at[0])
    part = cnt_row[0]
    for n in range(planes - 1):
        part = part + cnt_rows[n]
    part_row[0] = part
    for step in range(1, nz):
        send(part_row, part_rows.at[pl.ds(step - 1, 1)], 2, line_peers[step - 1])
    drain(rows, nt - 1, recv_sem.at[1])
    owner_row = lax.broadcasted_iota(jnp.int32, (nt, 128), 0)
    gathered = jnp.broadcast_to(own_row[0], (nt, 128))
    for n in range(nt - 1):
        gathered = jnp.where(owner_row == owners[n], jnp.broadcast_to(rows[n], (nt, 128)), gathered)
    gath_ref[...] = gathered
    drain(part_rows, nz - 1, recv_sem.at[2])
    total = part
    for n in range(nz - 1):
        total = total + part_rows[n]
    total_ref[...] = total
    drain(cnt_rows, planes - 1, send_sem.at[0])
    drain(rows, nt - 1, send_sem.at[1])
    drain(part_rows, nz - 1, send_sem.at[2])


def exchange(sizes, logp_new, logp_old, advantage, live_counts):
    plane_bits, line_bits, nt = sizes
    planes, nz = 1 << len(plane_bits), 1 << len(line_bits)
    own = logp_new.shape[0]
    f32 = jnp.float32
    any_spec = pl.BlockSpec(memory_space=pltpu.HBM)
    vmem = pl.BlockSpec(memory_space=pltpu.VMEM)
    return pl.pallas_call(
        functools.partial(exchange_kernel, plane_bits, line_bits, nt),
        out_shape=(jax.ShapeDtypeStruct((nt, 128), f32), jax.ShapeDtypeStruct((1, 128), f32)),
        in_specs=[any_spec] * 3 + [pl.BlockSpec(memory_space=pltpu.SMEM)],
        out_specs=(vmem, vmem),
        scratch_shapes=[
            pltpu.VMEM((1, own), f32),
            pltpu.VMEM((1, own), f32),
            pltpu.VMEM((1, own), f32),
            pltpu.VMEM((1, 1, 128), f32),
            pltpu.VMEM((nt - 1, 1, 128), f32),
            pltpu.VMEM((1, 1, 128), f32),
            pltpu.VMEM((planes - 1, 1, 128), f32),
            pltpu.VMEM((1, 1, 128), f32),
            pltpu.VMEM((nz - 1, 1, 128), f32),
            pltpu.SemaphoreType.DMA((4,)),
            pltpu.SemaphoreType.DMA((3,)),
            pltpu.SemaphoreType.DMA((3,)),
        ],
        compiler_params=pltpu.CompilerParams(collective_id=0, has_side_effects=True),
        name="exchange",
    )(*in_hbm(logp_new.reshape(1, own), logp_old.reshape(1, own), advantage.reshape(1, own)), live_counts)


def row_coefs(tokens, gath, total, seg_row, ver_row, caps, count):
    nt = gath.shape[0]
    rows = seg_row.shape[1]
    half = rows // nt
    bf16, f32 = jnp.bfloat16, jnp.float32
    lane = lax.broadcasted_iota(jnp.int32, (nt, 128), 1)
    other = pltpu.roll(gath, half, 1)
    ratio = jnp.where(lane < half, gath, other)
    adv = jnp.where(lane < half, other, gath)
    place = lax.broadcasted_iota(jnp.int32, (nt, rows), 1) // half
    mine = place == lax.broadcasted_iota(jnp.int32, (nt, rows), 0)
    copies = rows // 128
    ratio = jnp.where(mine, jnp.concatenate([ratio] * copies, axis=1), 0.0)
    adv = jnp.sum(jnp.where(mine, jnp.concatenate([adv] * copies, axis=1), 0.0), axis=0, keepdims=True)
    hi = ratio.astype(bf16).astype(f32)
    mid = (ratio - hi).astype(bf16).astype(f32)
    low = ratio - hi - mid
    ones = jnp.ones((nt, rows), f32)
    left = jnp.concatenate([hi, mid, low, ones], axis=0).astype(bf16)
    seg = seg_row.astype(f32)
    seg_col = jnp.broadcast_to(seg, (128, rows)).T
    sums = []
    for a in range(rows // 128):
        same = jnp.where(seg_col == seg[:, a * 128:(a + 1) * 128], 1.0, 0.0).astype(bf16)
        sums.append(jnp.dot(left, same, preferred_element_type=f32))
    sums = jnp.concatenate(sums, axis=1)
    seg_sum = jnp.sum(sums[:3 * nt], axis=0, keepdims=True)
    seg_len = sums[3 * nt:3 * nt + 1]
    cap = jnp.zeros((1, rows), f32)
    for n in range(caps.shape[0]):
        cap = jnp.where(ver_row == n, caps[n], cap)
    weight = jnp.minimum(jnp.exp(seg_sum / seg_len), cap)
    total = jnp.concatenate([total] * copies, axis=1)
    live = lax.broadcasted_iota(jnp.int32, (1, rows), 1) < count
    return jnp.where(live, -adv * weight * (tokens / total), 0.0)


def attend_kernel(tokens, cnt_s, gath_ref, total_ref, seq_hbm, caps_hbm, seq_row_hbm, seg_hbm, ver_hbm,
                  q_hbm, k_hbm, v_hbm, g_hbm, dq_hbm, dk_hbm, dv_hbm,
                  q, k, v, g, dq, dk, dv, probs_t, dscore_t, k_t, bias,
                  seq_s, caps_s, seq_ref, seg_ref, ver_ref, sems):
    rows, columns = q.shape
    heads = columns // HEAD_DIM
    tiles = rows // TILE
    bf16, f32 = jnp.bfloat16, jnp.float32
    scale = HEAD_DIM ** -0.5
    factor = scale * math.log2(math.e)

    def tile_rows(i):
        return pl.ds(i * TILE, TILE)

    k_in = pltpu.make_async_copy(k_hbm, k, sems.at[0])
    v_in = pltpu.make_async_copy(v_hbm, v, sems.at[1])
    q_in = [pltpu.make_async_copy(q_hbm.at[tile_rows(i)], q.at[tile_rows(i)], sems.at[2 + i]) for i in range(tiles)]
    g_in = [pltpu.make_async_copy(g_hbm.at[tile_rows(i)], g.at[tile_rows(i)], sems.at[2 + tiles + i])
            for i in range(tiles)]
    dq_out = [pltpu.make_async_copy(dq.at[tile_rows(i)], dq_hbm.at[tile_rows(i)], sems.at[2 + 2 * tiles + i])
              for i in range(tiles)]
    dv_out = pltpu.make_async_copy(dv, dv_hbm, sems.at[2 + 3 * tiles])
    dk_out = pltpu.make_async_copy(dk, dk_hbm, sems.at[3 + 3 * tiles])
    small = [
        pltpu.make_async_copy(src, dst, sems.at[4 + 3 * tiles + n])
        for n, (src, dst) in enumerate(((seq_hbm, seq_s), (caps_hbm, caps_s),
                                        (seq_row_hbm, seq_ref), (seg_hbm, seg_ref), (ver_hbm, ver_ref)))
    ]
    for load in small:
        load.start()
    k_in.start()
    v_in.start()
    for i in range(tiles):
        q_in[i].start()
        g_in[i].start()
    for load in small:
        load.wait()
    coef = row_coefs(tokens, gath_ref[...], total_ref[...], seg_ref[...], ver_ref[...], caps_s, cnt_s[0])
    k_in.wait()
    v_in.wait()
    k_t[...] = k[...].astype(f32).T.astype(bf16)

    def head_pair(ref, i, p):
        return jnp.concatenate(
            [ref[i * TILE:(i + 1) * TILE, (2 * p + n) * HEAD_DIM:(2 * p + n + 1) * HEAD_DIM] for n in range(2)],
            axis=0)

    contract_last = (((1,), (1,)), ((), ()))

    def body(first):
        for i in range(tiles):
            j0, j1 = first[i] * TILE, (i + 1) * TILE
            span = j1 - j0
            row_j = lax.broadcasted_iota(jnp.int32, (span, TILE), 0) + j0
            col_t = lax.broadcasted_iota(jnp.int32, (span, TILE), 1) + i * TILE
            begin = seq_ref[:, i * TILE:(i + 1) * TILE]
            bias[0:span, :] = jnp.where((row_j >= begin) & (row_j <= col_t), 0.0, NEG)
            q_in[i].wait()
            g_in[i].wait()
            coef_i = coef[:, i * TILE:(i + 1) * TILE]
            coef_pair = jnp.concatenate([coef_i, coef_i], axis=1)
            for p in range(heads // 2):
                scores = lax.dot_general(k[j0:j1, :], head_pair(q, i, p), contract_last, preferred_element_type=f32)
                d_prob = lax.dot_general(v[j0:j1, :], head_pair(g, i, p), contract_last, preferred_element_type=f32)
                scores = scores + jnp.concatenate([bias[0:span, :]] * 2, axis=1)
                top = jnp.max(scores, axis=0, keepdims=True)
                mass = jnp.exp2((scores - top) * factor)
                norm = 1.0 / jnp.sum(mass, axis=0, keepdims=True)
                delta = jnp.sum(mass * d_prob, axis=0, keepdims=True) * norm
                weighted = mass * (norm * coef_pair)
                lanes = slice(i * columns + 2 * p * TILE, i * columns + 2 * (p + 1) * TILE)
                probs_t[j0:j1, lanes] = weighted.astype(bf16)
                dscore_t[j0:j1, lanes] = (weighted * (d_prob - delta)).astype(bf16)
            dq_t = jnp.dot(k_t[:, j0:j1], dscore_t[j0:j1, i * columns:(i + 1) * columns],
                           preferred_element_type=f32) * scale
            for h in range(heads):
                dq[i * TILE:(i + 1) * TILE, h * HEAD_DIM:(h + 1) * HEAD_DIM] = (
                    dq_t[:, h * TILE:(h + 1) * TILE].T.astype(bf16))
            dq_out[i].start()
        for j in range(tiles):
            users = [i for i in range(j, tiles) if first[i] <= j]
            lanes = slice(users[0] * columns, (users[-1] + 1) * columns)
            stack = [(i, h) for i in users for h in range(heads)]
            for source, right, target, factor_out in ((probs_t, g, dv, None), (dscore_t, q, dk, scale)):
                stacked = jnp.concatenate(
                    [right[i * TILE:(i + 1) * TILE, h * HEAD_DIM:(h + 1) * HEAD_DIM] for i, h in stack], axis=0)
                value = jnp.dot(source[j * TILE:(j + 1) * TILE, lanes], stacked, preferred_element_type=f32)
                if factor_out is not None:
                    value = value * factor_out
                target[j * TILE:(j + 1) * TILE, :] = value.astype(bf16)

    dense = [0] * tiles
    band = [max(i - 1, 0) for i in range(tiles)]
    near = seq_s[0] >= 0
    for i in range(2, tiles):
        near = near & (seq_s[i * TILE] >= band[i] * TILE)

    @pl.when(near)
    def _():
        body(band)

    @pl.when(jnp.logical_not(near))
    def _():
        body(dense)

    dv_out.start()
    dk_out.start()
    for i in range(tiles):
        dq_out[i].wait()
    dv_out.wait()
    dk_out.wait()


def attend(tokens, gath, total, ratio_caps, live_counts, seq_begin, seg_begin, policy_version, q, k, v, g):
    rows, columns = q.shape
    tiles = rows // TILE
    bf16 = jnp.bfloat16
    vmem = pl.BlockSpec(memory_space=pltpu.VMEM)
    any_spec = pl.BlockSpec(memory_space=pltpu.HBM)
    wide, narrow = (rows, columns), (rows, HEAD_DIM)
    return pl.pallas_call(
        functools.partial(attend_kernel, tokens),
        out_shape=tuple(jax.ShapeDtypeStruct(s, bf16) for s in (wide, narrow, narrow)),
        in_specs=[pl.BlockSpec(memory_space=pltpu.SMEM)] + [vmem] * 2 + [any_spec] * 9,
        out_specs=(any_spec,) * 3,
        scratch_shapes=[
            pltpu.VMEM(wide, bf16),
            pltpu.VMEM(narrow, bf16),
            pltpu.VMEM(narrow, bf16),
            pltpu.VMEM(wide, bf16),
            pltpu.VMEM(wide, bf16),
            pltpu.VMEM(narrow, bf16),
            pltpu.VMEM(narrow, bf16),
            pltpu.VMEM((rows, tiles * columns), bf16),
            pltpu.VMEM((rows, tiles * columns), bf16),
            pltpu.VMEM((HEAD_DIM, rows), bf16),
            pltpu.VMEM((rows, TILE), jnp.float32),
            pltpu.SMEM((rows,), jnp.int32),
            pltpu.SMEM(ratio_caps.shape, jnp.float32),
            pltpu.VMEM((1, rows), jnp.int32),
            pltpu.VMEM((1, rows), jnp.int32),
            pltpu.VMEM((1, rows), jnp.int32),
            pltpu.SemaphoreType.DMA((10 + 3 * tiles,)),
        ],
        compiler_params=pltpu.CompilerParams(vmem_limit_bytes=40 * 2**20),
        name="attend",
    )(live_counts, gath, total, *in_hbm(seq_begin, ratio_caps, seq_begin.reshape(1, rows), seg_begin.reshape(1, rows),
                           policy_version.reshape(1, rows), q, k, v, g))


def solution(mesh):
    blocks, nt = mesh.shape["dp"], mesh.shape["tensor"]
    top = blocks.bit_length() - 1
    plane_bits, line_bits = (0, top - 2, top - 1), tuple(range(1, top - 2))

    def local(query_heads, key_heads, value_heads, logp_grad, logp_new, logp_old, advantage, ratio_caps,
              live_counts, seq_begin, seg_begin, policy_version):
        tokens = float(query_heads.shape[0] * blocks)
        gath, total = exchange((plane_bits, line_bits, nt), logp_new, logp_old, advantage, live_counts)
        return attend(tokens, gath, total, ratio_caps, live_counts, seq_begin, seg_begin, policy_version,
                      query_heads, key_heads, value_heads, logp_grad)

    row, every = P("dp"), P(("dp", "tensor"))
    both = P("dp", "tensor")
    return jax.shard_map(
        local,
        mesh=mesh,
        in_specs=(both, both, both, both, every, every, every, P(), row, row, row, row),
        out_specs=(both, both, both),
        check_vma=False,
    )
```

time: 442 us -> 37.7 us (0.09)
  the two profiles are of different devices: /device:TPU:70 before, /device:TPU:1 now
where the time goes in v1:
time: 37.7 us; the launch traced here: 37.5 us
  Pallas kernels  34.9 us (93%)
  local copies, waits for them, and re-layouts  1.31 us (3%)
  between operations  1.3 us (3%)
    pallas_call x1, Pallas kernels, exchange(): pl.pallas_call(functools.partial(exchange_kernel, plane_bits, line_bits,...  27.7 us
    pallas_call x1, Pallas kernels, attend(): pl.pallas_call(functools.partial(attend_kernel, tokens), out_shape=tuple(...  7.19 us
    unnamed x4, local copies, waits for them, and re-layouts  1.31 us

profile of v1, /device:TPU:1, one launch (start us, length us, event | category | flops | bytes accessed | tf_op | source)
XLA Modules:
  0.0 37.5 jit_solution(4245916217755232808)
XLA Ops:
  1.3 27.7 %exchange.1 = (f32[8,128]{1,0:T(8,128)}, f32[1,128]{1,0:T(1,128)}) custom-call(f32[1,64]{1,0:T(1,128)} %bitcast.9, f32[1,64]{1,0:T(1,128)} %bitcast.10, f32[1,64]{1,0:T(1,128)} %bitcast.11, s32[1]{0:T(128)S(6)} %copy.15.cnt_s), custom_call_target="tpu_custom_call" | custom-call | tf_op jit(solution)/shard_map/exchange/pallas_call | solution.py:108
  29.0 0.0 copy-start.1
  29.0 0.6 %copy-done.1 = f32[1,128]{1,0:T(1,128)S(1)} copy-done((f32[1,128]{1,0:T(1,128)S(1)}, f32[1,128]{1,0:T(1,128)}, u32[]{:S(2)}) %copy-start.1) | copy-done | bytes 536
  29.6 0.0 copy-start
  29.6 0.7 %copy-done = f32[8,128]{1,0:T(8,128)S(1)} copy-done((f32[8,128]{1,0:T(8,128)S(1)}, f32[8,128]{1,0:T(8,128)}, u32[]{:S(2)}) %copy-start) | copy-done | bytes 4120
  30.3 7.2 %attend.1 = (bf16[512,1024]{1,0:T(8,128)(2,1)}, bf16[512,128]{1,0:T(8,128)(2,1)}, bf16[512,128]{1,0:T(8,128)(2,1)}) custom-call(s32[1]{0:T(128)S(6)} %copy.15.cnt_s, f32[8,128]{1,0:T(8,128)S(1)} %copy-done, f32[1,128]{1,0:T(1,128)S(1)} %copy-done.1, s32[512]{0:T(512)} %seq_hbm.1, f32[4]{0:T(128)} %caps_hbm.1, s32[1,512]{1,0:T(1,128)} %bitcast.6, ...), custom_call_target="tpu_custom_call" | custom-call | tf_op jit(solution)/shard_map/attend/pallas_call | solution.py:289
Async XLA Ops:
  29.0 0.6 %copy-start.1 = (f32[1,128]{1,0:T(1,128)S(1)}, f32[1,128]{1,0:T(1,128)}, u32[]{:S(2)}) copy-start(f32[1,128]{1,0:T(1,128)} %get-tuple-element.6.total_ref) | copy-start | bytes 1540
  29.6 0.7 %copy-start = (f32[8,128]{1,0:T(8,128)S(1)}, f32[8,128]{1,0:T(8,128)}, u32[]{:S(2)}) copy-start(f32[8,128]{1,0:T(8,128)} %get-tuple-element.5.gath_ref) | copy-start | bytes 12292

commit v2 on v1

v2 whole, which is shorter than its diff:
```python
import functools
import math

import jax
import jax.numpy as jnp
from jax import lax
from jax.experimental import pallas as pl
from jax.experimental.pallas import tpu as pltpu
from jax.sharding import PartitionSpec as P

HEAD_DIM = 128
TILE = 128
MESH = pl.DeviceIdType.MESH
NEG = -1e30


def in_hbm(*arrays):
    return [pltpu.with_memory_space_constraint(a, pltpu.HBM) for a in arrays]


def flips(index, bits):
    return [(1 << b) * (1 - 2 * lax.rem(lax.div(index, 1 << b), 2)) for b in bits]


def partners(index, bits):
    deltas = flips(index, bits)
    found = []
    for mask in range(1, 1 << len(bits)):
        other = index
        for n, delta in enumerate(deltas):
            if mask >> n & 1:
                other = other + delta
        found.append(other)
    return found


def window_peers(dp, me, steps, z_lo_bits, tensor_half, z_all):
    low = 1 << len(z_lo_bits)
    unit = 1 << z_lo_bits[0]
    z_lo = lax.rem(lax.div(dp, unit), low)
    z_hi = lax.div(me, tensor_half)
    z = z_hi * low + z_lo
    found = []
    for step in steps:
        other = lax.rem(z + step + z_all, z_all)
        other_hi = lax.div(other, low)
        other_lo = other - other_hi * low
        found.append((dp + (other_lo - z_lo) * unit, me + (other_hi - z_hi) * tensor_half))
    return found


def segment_mask(seg_row):
    rows = seg_row.shape[1]
    seg = seg_row.astype(jnp.float32)
    seg_col = jnp.broadcast_to(seg, (128, rows)).T
    return [
        jnp.where(seg_col == seg[:, a * 128:(a + 1) * 128], 1.0, 0.0).astype(jnp.bfloat16) for a in range(rows // 128)
    ]


def row_coefs(tokens, gath, same, row_cap, count):
    nt = gath.shape[0]
    rows = row_cap.shape[1]
    half = rows // nt
    bf16, f32 = jnp.bfloat16, jnp.float32
    lane = lax.broadcasted_iota(jnp.int32, (nt, 128), 1)
    other = pltpu.roll(gath, half, 1)
    ratio = jnp.where(lane < half, gath, other)
    adv = jnp.where(lane < half, other, gath)
    place = lax.broadcasted_iota(jnp.int32, (nt, rows), 1) // half
    mine = place == lax.broadcasted_iota(jnp.int32, (nt, rows), 0)
    copies = rows // 128
    ratio = jnp.where(mine, jnp.concatenate([ratio] * copies, axis=1), 0.0)
    adv = jnp.sum(jnp.where(mine, jnp.concatenate([adv] * copies, axis=1), 0.0), axis=0, keepdims=True)
    hi = ratio.astype(bf16).astype(f32)
    mid = (ratio - hi).astype(bf16).astype(f32)
    low = ratio - hi - mid
    ones = jnp.ones((nt, rows), f32)
    left = jnp.concatenate([hi, mid, low, ones], axis=0).astype(bf16)
    sums = jnp.dot(left, same, preferred_element_type=f32)
    seg_sum = jnp.sum(sums[:3 * nt], axis=0, keepdims=True)
    seg_len = sums[3 * nt:3 * nt + 1]
    weight = jnp.minimum(jnp.exp(seg_sum / seg_len), row_cap)
    live = lax.broadcasted_iota(jnp.int32, (1, rows), 1) < count
    return jnp.where(live, -adv * weight * tokens, 0.0)


def block_kernel(tokens, plane_bits, z_lo_bits, z_all, nt, cnt_s,
                 new_hbm, old_hbm, adv_hbm, caps_hbm, seq_hbm, seg_hbm, ver_hbm, q_hbm, k_hbm, v_hbm, g_hbm,
                 dq_hbm, dk_ref, dv_ref, coef_ref,
                 q, k, v, g, dq, cq, cg, probs_t, dscore_t, k_t, bias, same, row_cap, dk_sum, dv_sum,
                 caps_s, seq_ref, seg_ref, ver_ref,
                 new_v, old_v, adv_v, own_row, rows_in, cnt_row, cnt_rows, part_row, part_rows,
                 sems, load_sem, send_sem, recv_sem):
    rows, columns = q.shape
    heads = columns // HEAD_DIM
    tiles = rows // TILE
    bf16, f32 = jnp.bfloat16, jnp.float32
    scale = HEAD_DIM ** -0.5
    factor = scale * math.log2(math.e)

    dp = lax.axis_index("dp")
    me = lax.axis_index("tensor")
    owners = partners(me, range(nt.bit_length() - 1))
    tensor_peers = [(dp, t) for t in owners]
    plane_peers = [(d, me) for d in partners(dp, plane_bits)]
    low = 1 << len(z_lo_bits)
    steps = [n for n in range(1 - low // 2, low // 2 + 1) if n != 0]
    from_window = window_peers(dp, me, steps, z_lo_bits, nt // 2, z_all)
    to_window = window_peers(dp, me, [-n for n in steps], z_lo_bits, nt // 2, z_all)
    planes = len(plane_peers) + 1

    barrier = pltpu.get_barrier_semaphore()
    for peer in tensor_peers + plane_peers + from_window:
        pl.semaphore_signal(barrier, inc=1, device_id=peer, device_id_type=MESH)

    def start_all(pairs, sem, first):
        copies = [pltpu.make_async_copy(src, dst, sem.at[first + n]) for n, (src, dst) in enumerate(pairs)]
        for copy in copies:
            copy.start()
        return copies

    def tile_rows(i):
        return pl.ds(i * TILE, TILE)

    own_in = start_all(((new_hbm, new_v), (old_hbm, old_v), (adv_hbm, adv_v)), load_sem, 0)
    small_in = start_all(((seq_hbm, seq_ref), (seg_hbm, seg_ref), (ver_hbm, ver_ref), (caps_hbm, caps_s),
                          (k_hbm, k), (v_hbm, v)), sems, 0)
    wide_in = [start_all(((q_hbm.at[tile_rows(i)], q.at[tile_rows(i)]), (g_hbm.at[tile_rows(i)], g.at[tile_rows(i)])),
                         sems, 6 + 2 * i) for i in range(tiles)]
    dq_out = [pltpu.make_async_copy(dq.at[tile_rows(i)], dq_hbm.at[tile_rows(i)], sems.at[6 + 2 * tiles + i])
              for i in range(tiles)]

    def send(src, dst, n, peer):
        pltpu.make_async_remote_copy(
            src_ref=src, dst_ref=dst, send_sem=send_sem.at[n], recv_sem=recv_sem.at[n],
            device_id=peer, device_id_type=MESH).start()

    def drain(buffer, n, sem):
        span = buffer.at[pl.ds(0, n)]
        pltpu.make_async_copy(span, span, sem).wait()

    def communicate():
        for load in own_in:
            load.wait()
        own_row[0] = jnp.concatenate([new_v[...] - old_v[...], adv_v[...]], axis=1)
        cnt_row[0] = jnp.full((1, 128), cnt_s[0].astype(f32), f32)
        pl.semaphore_wait(barrier, len(tensor_peers) + len(plane_peers) + len(to_window))
        for n, peer in enumerate(tensor_peers):
            send(own_row, rows_in.at[pl.ds(n, 1)], 1, peer)
        for n, peer in enumerate(plane_peers):
            send(cnt_row, cnt_rows.at[pl.ds(n, 1)], 0, peer)
        drain(cnt_rows, planes - 1, recv_sem.at[0])
        part = cnt_row[0]
        for n in range(planes - 1):
            part = part + cnt_rows[n]
        part_row[0] = part
        for n, peer in enumerate(to_window):
            send(part_row, part_rows.at[pl.ds(n, 1)], 2, peer)

    def head_pair(ref, i, p):
        return jnp.concatenate(
            [ref[i * TILE:(i + 1) * TILE, (2 * p + n) * HEAD_DIM:(2 * p + n + 1) * HEAD_DIM] for n in range(2)],
            axis=0)

    contract_last = (((1,), (1,)), ((), ()))
    far = me >= nt // 2

    @pl.when(far)
    def _():
        communicate()

    for load in small_in:
        load.wait()
    cap = jnp.zeros((1, rows), f32)
    for n in range(caps_s.shape[0]):
        cap = jnp.where(ver_ref[...] == n, caps_s[n], cap)
    row_cap[...] = cap
    for a, part in enumerate(segment_mask(seg_ref[...])):
        same[:, a * 128:(a + 1) * 128] = part
    k_t[...] = k[...].astype(f32).T.astype(bf16)
    for i in range(tiles):
        span = (i + 1) * TILE
        row_j = lax.broadcasted_iota(jnp.int32, (span, TILE), 0)
        col_t = lax.broadcasted_iota(jnp.int32, (span, TILE), 1) + i * TILE
        begin = seq_ref[:, i * TILE:(i + 1) * TILE]
        bias[0:span, :] = jnp.where((row_j >= begin) & (row_j <= col_t), 0.0, NEG)
        for load in wide_in[i]:
            load.wait()
        for p in range(heads // 2):
            scores = lax.dot_general(k[0:span, :], head_pair(q, i, p), contract_last, preferred_element_type=f32)
            d_prob = lax.dot_general(v[0:span, :], head_pair(g, i, p), contract_last, preferred_element_type=f32)
            scores = scores + jnp.concatenate([bias[0:span, :]] * 2, axis=1)
            top = jnp.max(scores, axis=0, keepdims=True)
            mass = jnp.exp2((scores - top) * factor)
            norm = 1.0 / jnp.sum(mass, axis=0, keepdims=True)
            delta = jnp.sum(mass * d_prob, axis=0, keepdims=True) * norm
            probs = mass * norm
            lanes = slice(i * columns + 2 * p * TILE, i * columns + 2 * (p + 1) * TILE)
            probs_t[0:span, lanes] = probs.astype(bf16)
            dscore_t[0:span, lanes] = (probs * (d_prob - delta)).astype(bf16)
        dq_t = jnp.dot(k_t[:, 0:span], dscore_t[0:span, i * columns:(i + 1) * columns],
                       preferred_element_type=f32) * scale
        for h in range(heads):
            dq[i * TILE:(i + 1) * TILE, h * HEAD_DIM:(h + 1) * HEAD_DIM] = (
                dq_t[:, h * TILE:(h + 1) * TILE].T.astype(bf16))
        dq_out[i].start()

    @pl.when(jnp.logical_not(far))
    def _():
        communicate()

    drain(rows_in, nt - 1, recv_sem.at[1])
    owner_row = lax.broadcasted_iota(jnp.int32, (nt, 128), 0)
    gathered = jnp.broadcast_to(own_row[0], (nt, 128))
    for n in range(nt - 1):
        gathered = jnp.where(owner_row == owners[n], jnp.broadcast_to(rows_in[n], (nt, 128)), gathered)
    coef = row_coefs(tokens, gathered, same[...], row_cap[...], cnt_s[0])
    coef_col = jnp.broadcast_to(coef, (HEAD_DIM, rows)).T
    for h in range(heads):
        lanes = slice(h * HEAD_DIM, (h + 1) * HEAD_DIM)
        cg[:, lanes] = (g[:, lanes].astype(f32) * coef_col).astype(bf16)
        cq[:, lanes] = (q[:, lanes].astype(f32) * coef_col).astype(bf16)
    for j in range(tiles):
        lanes = slice(j * columns, tiles * columns)
        stack = [(i, h) for i in range(j, tiles) for h in range(heads)]
        for source, right, target in ((probs_t, cg, dv_sum), (dscore_t, cq, dk_sum)):
            stacked = jnp.concatenate(
                [right[i * TILE:(i + 1) * TILE, h * HEAD_DIM:(h + 1) * HEAD_DIM] for i, h in stack], axis=0)
            target[j * TILE:(j + 1) * TILE, :] = jnp.dot(
                source[j * TILE:(j + 1) * TILE, lanes], stacked, preferred_element_type=f32)
    drain(part_rows, low - 1, recv_sem.at[2])
    total = part_row[0]
    for n in range(low - 1):
        total = total + part_rows[n]
    inverse = jnp.where(total > 0.0, 1.0 / total, 0.0)
    coef_ref[...] = coef * jnp.concatenate([inverse] * (rows // 128), axis=1)
    dv_ref[...] = (dv_sum[...] * inverse).astype(bf16)
    dk_ref[...] = (dk_sum[...] * (inverse * scale)).astype(bf16)
    drain(rows_in, nt - 1, send_sem.at[1])
    drain(cnt_rows, planes - 1, send_sem.at[0])
    drain(part_rows, low - 1, send_sem.at[2])
    for i in range(tiles):
        dq_out[i].wait()


def block(tokens, bits, nt, cnt, logp_new, logp_old, advantage, caps, seq_begin, seg_begin, version, q, k, v, g):
    plane_bits, z_lo_bits, z_all = bits
    rows, columns = q.shape
    own = logp_new.shape[0]
    tiles = rows // TILE
    planes, low = 1 << len(plane_bits), 1 << len(z_lo_bits)
    bf16, f32, i32 = jnp.bfloat16, jnp.float32, jnp.int32
    hbm = pl.BlockSpec(memory_space=pltpu.HBM)
    vmem = pl.BlockSpec(memory_space=pltpu.VMEM)
    wide, narrow = (rows, columns), (rows, HEAD_DIM)
    dma = pltpu.SemaphoreType.DMA
    return pl.pallas_call(
        functools.partial(block_kernel, tokens, plane_bits, z_lo_bits, z_all, nt),
        out_shape=(jax.ShapeDtypeStruct(wide, bf16), jax.ShapeDtypeStruct(narrow, bf16),
                   jax.ShapeDtypeStruct(narrow, bf16), jax.ShapeDtypeStruct((1, rows), f32)),
        in_specs=[pl.BlockSpec(memory_space=pltpu.SMEM)] + [hbm] * 11,
        out_specs=(hbm, vmem, vmem, vmem),
        scratch_shapes=[
            pltpu.VMEM(wide, bf16), pltpu.VMEM(narrow, bf16), pltpu.VMEM(narrow, bf16), pltpu.VMEM(wide, bf16),
            pltpu.VMEM(wide, bf16), pltpu.VMEM(wide, bf16), pltpu.VMEM(wide, bf16),
            pltpu.VMEM((rows, tiles * columns), bf16), pltpu.VMEM((rows, tiles * columns), bf16),
            pltpu.VMEM((HEAD_DIM, rows), bf16), pltpu.VMEM((rows, TILE), f32),
            pltpu.VMEM((rows, rows), bf16), pltpu.VMEM((1, rows), f32),
            pltpu.VMEM(narrow, f32), pltpu.VMEM(narrow, f32),
            pltpu.SMEM(caps.shape, f32),
            pltpu.VMEM((1, rows), i32), pltpu.VMEM((1, rows), i32), pltpu.VMEM((1, rows), i32),
            pltpu.VMEM((1, own), f32), pltpu.VMEM((1, own), f32), pltpu.VMEM((1, own), f32),
            pltpu.VMEM((1, 1, 128), f32), pltpu.VMEM((nt - 1, 1, 128), f32),
            pltpu.VMEM((1, 1, 128), f32), pltpu.VMEM((planes - 1, 1, 128), f32),
            pltpu.VMEM((1, 1, 128), f32), pltpu.VMEM((low - 1, 1, 128), f32),
            dma((6 + 3 * tiles,)), dma((3,)), dma((3,)), dma((3,)),
        ],
        compiler_params=pltpu.CompilerParams(
            collective_id=0, has_side_effects=True, vmem_limit_bytes=58 * 2**20),
        name="block",
    )(cnt, *in_hbm(logp_new.reshape(1, own), logp_old.reshape(1, own), advantage.reshape(1, own), caps,
                   seq_begin.reshape(1, rows), seg_begin.reshape(1, rows), version.reshape(1, rows), q, k, v, g))


def finish_kernel(coef_hbm, dq_in, dk_in, dv_in, dq_hbm, dk_hbm, dv_hbm, coef, dq, sems):
    rows, columns = dq.shape
    tiles = rows // TILE
    coef_load = pltpu.make_async_copy(coef_hbm, coef, sems.at[0])
    passed = [pltpu.make_async_copy(dk_in, dk_hbm, sems.at[1]), pltpu.make_async_copy(dv_in, dv_hbm, sems.at[2])]
    loads = [pltpu.make_async_copy(dq_in.at[pl.ds(i * TILE, TILE)], dq.at[pl.ds(i * TILE, TILE)], sems.at[3 + i])
             for i in range(tiles)]
    stores = [pltpu.make_async_copy(dq.at[pl.ds(i * TILE, TILE)], dq_hbm.at[pl.ds(i * TILE, TILE)],
                                    sems.at[3 + tiles + i]) for i in range(tiles)]
    for copy in [coef_load] + loads + passed:
        copy.start()
    coef_load.wait()
    coef_col = jnp.broadcast_to(coef[...], (HEAD_DIM, rows)).T
    for i in range(tiles):
        here = slice(i * TILE, (i + 1) * TILE)
        loads[i].wait()
        for h in range(columns // HEAD_DIM):
            lanes = slice(h * HEAD_DIM, (h + 1) * HEAD_DIM)
            dq[here, lanes] = (dq[here, lanes].astype(jnp.float32) * coef_col[here]).astype(dq.dtype)
        stores[i].start()
    for copy in stores + passed:
        copy.wait()


def finish(coef, dq, dk, dv):
    hbm = pl.BlockSpec(memory_space=pltpu.HBM)
    rows = dq.shape[0]
    return pl.pallas_call(
        finish_kernel,
        out_shape=tuple(jax.ShapeDtypeStruct(a.shape, a.dtype) for a in (dq, dk, dv)),
        in_specs=[hbm] * 4,
        out_specs=(hbm,) * 3,
        scratch_shapes=[pltpu.VMEM(coef.shape, jnp.float32), pltpu.VMEM(dq.shape, dq.dtype),
                        pltpu.SemaphoreType.DMA((3 + 2 * (rows // TILE),))],
        compiler_params=pltpu.CompilerParams(vmem_limit_bytes=58 * 2**20),
        name="finish",
    )(*in_hbm(coef, dq, dk, dv))


def solution(mesh):
    blocks, nt = mesh.shape["dp"], mesh.shape["tensor"]
    top = blocks.bit_length() - 1
    plane_bits, z_lo_bits = (0, top - 2, top - 1), tuple(range(1, top - 2))
    bits = (plane_bits, z_lo_bits, 2 << len(z_lo_bits))

    def local(query_heads, key_heads, value_heads, logp_grad, logp_new, logp_old, advantage, ratio_caps,
              live_counts, seq_begin, seg_begin, policy_version):
        tokens = float(query_heads.shape[0] * blocks)
        dq, dk, dv, coef = block(tokens, bits, nt, live_counts, logp_new, logp_old, advantage, ratio_caps,
                                 seq_begin, seg_begin, policy_version, query_heads, key_heads, value_heads, logp_grad)
        return finish(coef, dq, dk, dv)

    row, every = P("dp"), P(("dp", "tensor"))
    both = P("dp", "tensor")
    return jax.shard_map(
        local,
        mesh=mesh,
        in_specs=(both, both, both, both, every, every, every, P(), row, row, row, row),
        out_specs=(both, both, both),
        check_vma=False,
    )
```

time: 37.7 us -> 37.3 us (0.989)
  local copies, waits for them, and re-layouts: 1.31 us -> 0 us
  Pallas kernels: 34.9 us -> 35.8 us
    unnamed x4 -> x0, local copies, waits for them, and re-layouts: 1.31 us -> none
    pallas_call x2, Pallas kernels: 34.9 us -> 35.8 us  [the longest x1 26.7 us: block(): pl.pallas_call(functools.partial(block_kernel, tokens, plane_bits, z_lo_b...]
where the time goes in v2:
time: 37.3 us; the launch traced here: 37.1 us
  Pallas kernels  35.8 us (96%)
  between operations  1.29 us (3%)
    pallas_call x1, Pallas kernels, block(): pl.pallas_call(functools.partial(block_kernel, tokens, plane_bits, z_lo_b...  26.7 us
    pallas_call x1, Pallas kernels, finish(): pl.pallas_call(finish_kernel, out_shape=tuple((jax.ShapeDtypeStruct(a.sha...  9.15 us

profile of v2, /device:TPU:1, one launch (start us, length us, event | category | flops | bytes accessed | tf_op | source)
XLA Modules:
  0.0 37.1 jit_solution(8470355827856750735)
XLA Ops:
  1.3 26.7 %block.1 = (bf16[512,1024]{1,0:T(8,128)(2,1)}, bf16[512,128]{1,0:T(8,128)(2,1)}, bf16[512,128]{1,0:T(8,128)(2,1)}, f32[1,512]{1,0:T(1,128)}) custom-call(s32[1]{0:T(128)S(6)} %copy.15.cnt_s, f32[1,64]{1,0:T(1,128)} %bitcast.9, f32[1,64]{1,0:T(1,128)} %bitcast.10, f32[1,64]{1,0:T(1,128)} %bitcast.11, f32[4]{0:T(128)} %caps_hbm.1, s32[1,512]{1,0:T(1,128)} %bitcast.6, ...), custom_call_target="tpu_custom_call" | custom-call | tf_op jit(solution)/shard_map/block/pallas_call | solution.py:258
  28.0 9.1 %finish.1 = (bf16[512,1024]{1,0:T(8,128)(2,1)}, bf16[512,128]{1,0:T(8,128)(2,1)}, bf16[512,128]{1,0:T(8,128)(2,1)}) custom-call(f32[1,512]{1,0:T(1,128)} %get-tuple-element.7.coef_hbm, bf16[512,1024]{1,0:T(8,128)(2,1)} %get-tuple-element.8.dq_in, bf16[512,128]{1,0:T(8,128)(2,1)} %get-tuple-element.9.dk_in, bf16[512,128]{1,0:T(8,128)(2,1)} %get-tuple-element.10.dv_in), custom_call_target="tpu_custom_call" | custom-call | tf_op jit(solution)/shard_map/finish/pallas_call | solution.py:313

commit v3 on v2

--- a/solution.py
+++ b/solution.py
@@ -31,21 +31,6 @@
             if mask >> n & 1:
                 other = other + delta
         found.append(other)
-    return found
-
-
-def window_peers(dp, me, steps, z_lo_bits, tensor_half, z_all):
-    low = 1 << len(z_lo_bits)
-    unit = 1 << z_lo_bits[0]
-    z_lo = lax.rem(lax.div(dp, unit), low)
-    z_hi = lax.div(me, tensor_half)
-    z = z_hi * low + z_lo
-    found = []
-    for step in steps:
-        other = lax.rem(z + step + z_all, z_all)
-        other_hi = lax.div(other, low)
-        other_lo = other - other_hi * low
-        found.append((dp + (other_lo - z_lo) * unit, me + (other_hi - z_hi) * tensor_half))
     return found
 
 
@@ -85,12 +70,12 @@
     return jnp.where(live, -adv * weight * tokens, 0.0)
 
 
-def block_kernel(tokens, plane_bits, z_lo_bits, z_all, nt, cnt_s,
+def block_kernel(tokens, plane_bits, line_bits, nt, cnt_s,
                  new_hbm, old_hbm, adv_hbm, caps_hbm, seq_hbm, seg_hbm, ver_hbm, q_hbm, k_hbm, v_hbm, g_hbm,
-                 dq_hbm, dk_ref, dv_ref, coef_ref,
-                 q, k, v, g, dq, cq, cg, probs_t, dscore_t, k_t, bias, same, row_cap, dk_sum, dv_sum,
+                 dq, dk_ref, dv_ref, coef_ref,
+                 q, k, v, g, cq, cg, probs_t, dscore_t, k_t, bias, same, row_cap, dk_sum, dv_sum,
                  caps_s, seq_ref, seg_ref, ver_ref,
-                 new_v, old_v, adv_v, own_row, rows_in, cnt_row, cnt_rows, part_row, part_rows,
+                 new_v, old_v, adv_v, own_row, rows_in, cnt_row, cnt_rows, part_row, part_rows, total_row,
                  sems, load_sem, send_sem, recv_sem):
     rows, columns = q.shape
     heads = columns // HEAD_DIM
@@ -104,15 +89,28 @@
     owners = partners(me, range(nt.bit_length() - 1))
     tensor_peers = [(dp, t) for t in owners]
     plane_peers = [(d, me) for d in partners(dp, plane_bits)]
-    low = 1 << len(z_lo_bits)
-    steps = [n for n in range(1 - low // 2, low // 2 + 1) if n != 0]
-    from_window = window_peers(dp, me, steps, z_lo_bits, nt // 2, z_all)
-    to_window = window_peers(dp, me, [-n for n in steps], z_lo_bits, nt // 2, z_all)
-    planes = len(plane_peers) + 1
+    half = nt // 2
+    far = me >= half
+    near = me < half
+    line = [dp] + partners(dp, line_bits)
+    far_line = [(d, me + half) for d in line]
+    near_line = [(d, me - half) for d in line]
 
     barrier = pltpu.get_barrier_semaphore()
-    for peer in tensor_peers + plane_peers + from_window:
-        pl.semaphore_signal(barrier, inc=1, device_id=peer, device_id_type=MESH)
+
+    def greet(peers):
+        for peer in peers:
+            pl.semaphore_signal(barrier, inc=1, device_id=peer, device_id_type=MESH)
+
+    greet(tensor_peers)
+
+    @pl.when(far)
+    def _():
+        greet(plane_peers)
+
+    @pl.when(near)
+    def _():
+        greet(far_line[1:])
 
     def start_all(pairs, sem, first):
         copies = [pltpu.make_async_copy(src, dst, sem.at[first + n]) for n, (src, dst) in enumerate(pairs)]
@@ -128,9 +126,6 @@
                           (k_hbm, k), (v_hbm, v)), sems, 0)
     wide_in = [start_all(((q_hbm.at[tile_rows(i)], q.at[tile_rows(i)]), (g_hbm.at[tile_rows(i)], g.at[tile_rows(i)])),
                          sems, 6 + 2 * i) for i in range(tiles)]
-    dq_out = [pltpu.make_async_copy(dq.at[tile_rows(i)], dq_hbm.at[tile_rows(i)], sems.at[6 + 2 * tiles + i])
-              for i in range(tiles)]
-
     def send(src, dst, n, peer):
         pltpu.make_async_remote_copy(
             src_ref=src, dst_ref=dst, send_sem=send_sem.at[n], recv_sem=recv_sem.at[n],
@@ -140,23 +135,32 @@
         span = buffer.at[pl.ds(0, n)]
         pltpu.make_async_copy(span, span, sem).wait()
 
-    def communicate():
+    def send_rows(signals):
         for load in own_in:
             load.wait()
         own_row[0] = jnp.concatenate([new_v[...] - old_v[...], adv_v[...]], axis=1)
-        cnt_row[0] = jnp.full((1, 128), cnt_s[0].astype(f32), f32)
-        pl.semaphore_wait(barrier, len(tensor_peers) + len(plane_peers) + len(to_window))
+        pl.semaphore_wait(barrier, signals)
         for n, peer in enumerate(tensor_peers):
-            send(own_row, rows_in.at[pl.ds(n, 1)], 1, peer)
+            send(own_row, rows_in.at[pl.ds(n, 1)], 0, peer)
+
+    def send_partial():
         for n, peer in enumerate(plane_peers):
-            send(cnt_row, cnt_rows.at[pl.ds(n, 1)], 0, peer)
-        drain(cnt_rows, planes - 1, recv_sem.at[0])
+            send(cnt_row, cnt_rows.at[pl.ds(n, 1)], 1, peer)
+        drain(cnt_rows, len(plane_peers), recv_sem.at[1])
         part = cnt_row[0]
-        for n in range(planes - 1):
+        for n in range(len(plane_peers)):
             part = part + cnt_rows[n]
         part_row[0] = part
-        for n, peer in enumerate(to_window):
+        for n, peer in enumerate(near_line):
             send(part_row, part_rows.at[pl.ds(n, 1)], 2, peer)
+
+    def send_total():
+        drain(part_rows, len(line), recv_sem.at[2])
+        total = part_rows[0]
+        for n in range(1, len(line)):
+            total = total + part_rows[n]
+        total_row[0] = total
+        send(total_row, total_row, 3, far_line[0])
 
     def head_pair(ref, i, p):
         return jnp.concatenate(
@@ -164,11 +168,12 @@
             axis=0)
 
     contract_last = (((1,), (1,)), ((), ()))
-    far = me >= nt // 2
 
     @pl.when(far)
     def _():
-        communicate()
+        cnt_row[0] = jnp.full((1, 128), cnt_s[0].astype(f32), f32)
+        send_rows(len(tensor_peers) + len(plane_peers) + len(line) - 1)
+        send_partial()
 
     for load in small_in:
         load.wait()
@@ -204,18 +209,22 @@
         for h in range(heads):
             dq[i * TILE:(i + 1) * TILE, h * HEAD_DIM:(h + 1) * HEAD_DIM] = (
                 dq_t[:, h * TILE:(h + 1) * TILE].T.astype(bf16))
-        dq_out[i].start()
-
-    @pl.when(jnp.logical_not(far))
-    def _():
-        communicate()
-
-    drain(rows_in, nt - 1, recv_sem.at[1])
+
+    @pl.when(near)
+    def _():
+        send_rows(len(tensor_peers))
+
+    drain(rows_in, nt - 1, recv_sem.at[0])
     owner_row = lax.broadcasted_iota(jnp.int32, (nt, 128), 0)
     gathered = jnp.broadcast_to(own_row[0], (nt, 128))
     for n in range(nt - 1):
         gathered = jnp.where(owner_row == owners[n], jnp.broadcast_to(rows_in[n], (nt, 128)), gathered)
     coef = row_coefs(tokens, gathered, same[...], row_cap[...], cnt_s[0])
+
+    @pl.when(near)
+    def _():
+        send_total()
+
     coef_col = jnp.broadcast_to(coef, (HEAD_DIM, rows)).T
     for h in range(heads):
         lanes = slice(h * HEAD_DIM, (h + 1) * HEAD_DIM)
@@ -229,41 +238,48 @@
                 [right[i * TILE:(i + 1) * TILE, h * HEAD_DIM:(h + 1) * HEAD_DIM] for i, h in stack], axis=0)
             target[j * TILE:(j + 1) * TILE, :] = jnp.dot(
                 source[j * TILE:(j + 1) * TILE, lanes], stacked, preferred_element_type=f32)
-    drain(part_rows, low - 1, recv_sem.at[2])
-    total = part_row[0]
-    for n in range(low - 1):
-        total = total + part_rows[n]
+
+    @pl.when(far)
+    def _():
+        drain(total_row, 1, recv_sem.at[3])
+
+    total = total_row[0]
     inverse = jnp.where(total > 0.0, 1.0 / total, 0.0)
     coef_ref[...] = coef * jnp.concatenate([inverse] * (rows // 128), axis=1)
     dv_ref[...] = (dv_sum[...] * inverse).astype(bf16)
     dk_ref[...] = (dk_sum[...] * (inverse * scale)).astype(bf16)
-    drain(rows_in, nt - 1, send_sem.at[1])
-    drain(cnt_rows, planes - 1, send_sem.at[0])
-    drain(part_rows, low - 1, send_sem.at[2])
-    for i in range(tiles):
-        dq_out[i].wait()
+    drain(rows_in, nt - 1, send_sem.at[0])
+
+    @pl.when(far)
+    def _():
+        drain(cnt_rows, len(plane_peers), send_sem.at[1])
+        drain(part_rows, len(line), send_sem.at[2])
+
+    @pl.when(near)
+    def _():
+        drain(total_row, 1, send_sem.at[3])
 
 
 def block(tokens, bits, nt, cnt, logp_new, logp_old, advantage, caps, seq_begin, seg_begin, version, q, k, v, g):
-    plane_bits, z_lo_bits, z_all = bits
+    plane_bits, line_bits = bits
     rows, columns = q.shape
     own = logp_new.shape[0]
     tiles = rows // TILE
-    planes, low = 1 << len(plane_bits), 1 << len(z_lo_bits)
+    planes, low = 1 << len(plane_bits), 1 << len(line_bits)
     bf16, f32, i32 = jnp.bfloat16, jnp.float32, jnp.int32
     hbm = pl.BlockSpec(memory_space=pltpu.HBM)
     vmem = pl.BlockSpec(memory_space=pltpu.VMEM)
     wide, narrow = (rows, columns), (rows, HEAD_DIM)
     dma = pltpu.SemaphoreType.DMA
     return pl.pallas_call(
-        functools.partial(block_kernel, tokens, plane_bits, z_lo_bits, z_all, nt),
+        functools.partial(block_kernel, tokens, plane_bits, line_bits, nt),
         out_shape=(jax.ShapeDtypeStruct(wide, bf16), jax.ShapeDtypeStruct(narrow, bf16),
                    jax.ShapeDtypeStruct(narrow, bf16), jax.ShapeDtypeStruct((1, rows), f32)),
         in_specs=[pl.BlockSpec(memory_space=pltpu.SMEM)] + [hbm] * 11,
-        out_specs=(hbm, vmem, vmem, vmem),
+        out_specs=(vmem,) * 4,
         scratch_shapes=[
             pltpu.VMEM(wide, bf16), pltpu.VMEM(narrow, bf16), pltpu.VMEM(narrow, bf16), pltpu.VMEM(wide, bf16),
-            pltpu.VMEM(wide, bf16), pltpu.VMEM(wide, bf16), pltpu.VMEM(wide, bf16),
+            pltpu.VMEM(wide, bf16), pltpu.VMEM(wide, bf16),
             pltpu.VMEM((rows, tiles * columns), bf16), pltpu.VMEM((rows, tiles * columns), bf16),
             pltpu.VMEM((HEAD_DIM, rows), bf16), pltpu.VMEM((rows, TILE), f32),
             pltpu.VMEM((rows, rows), bf16), pltpu.VMEM((1, rows), f32),
@@ -273,35 +289,30 @@
             pltpu.VMEM((1, own), f32), pltpu.VMEM((1, own), f32), pltpu.VMEM((1, own), f32),
             pltpu.VMEM((1, 1, 128), f32), pltpu.VMEM((nt - 1, 1, 128), f32),
             pltpu.VMEM((1, 1, 128), f32), pltpu.VMEM((planes - 1, 1, 128), f32),
-            pltpu.VMEM((1, 1, 128), f32), pltpu.VMEM((low - 1, 1, 128), f32),
-            dma((6 + 3 * tiles,)), dma((3,)), dma((3,)), dma((3,)),
+            pltpu.VMEM((1, 1, 128), f32), pltpu.VMEM((low, 1, 128), f32), pltpu.VMEM((1, 1, 128), f32),
+            dma((6 + 2 * tiles,)), dma((3,)), dma((4,)), dma((4,)),
         ],
         compiler_params=pltpu.CompilerParams(
-            collective_id=0, has_side_effects=True, vmem_limit_bytes=58 * 2**20),
+            collective_id=0, has_side_effects=True, vmem_limit_bytes=32 * 2**20),
         name="block",
     )(cnt, *in_hbm(logp_new.reshape(1, own), logp_old.reshape(1, own), advantage.reshape(1, own), caps,
                    seq_begin.reshape(1, rows), seg_begin.reshape(1, rows), version.reshape(1, rows), q, k, v, g))
 
 
-def finish_kernel(coef_hbm, dq_in, dk_in, dv_in, dq_hbm, dk_hbm, dv_hbm, coef, dq, sems):
+def finish_kernel(coef, dq_in, dk_in, dv_in, dq_hbm, dk_hbm, dv_hbm, dq, sems):
     rows, columns = dq.shape
     tiles = rows // TILE
-    coef_load = pltpu.make_async_copy(coef_hbm, coef, sems.at[0])
-    passed = [pltpu.make_async_copy(dk_in, dk_hbm, sems.at[1]), pltpu.make_async_copy(dv_in, dv_hbm, sems.at[2])]
-    loads = [pltpu.make_async_copy(dq_in.at[pl.ds(i * TILE, TILE)], dq.at[pl.ds(i * TILE, TILE)], sems.at[3 + i])
-             for i in range(tiles)]
-    stores = [pltpu.make_async_copy(dq.at[pl.ds(i * TILE, TILE)], dq_hbm.at[pl.ds(i * TILE, TILE)],
-                                    sems.at[3 + tiles + i]) for i in range(tiles)]
-    for copy in [coef_load] + loads + passed:
+    passed = [pltpu.make_async_copy(dk_in, dk_hbm, sems.at[0]), pltpu.make_async_copy(dv_in, dv_hbm, sems.at[1])]
+    stores = [pltpu.make_async_copy(dq.at[pl.ds(i * TILE, TILE)], dq_hbm.at[pl.ds(i * TILE, TILE)], sems.at[2 + i])
+              for i in range(tiles)]
+    for copy in passed:
         copy.start()
-    coef_load.wait()
-    coef_col = jnp.broadcast_to(coef[...], (HEAD_DIM, rows)).T
     for i in range(tiles):
         here = slice(i * TILE, (i + 1) * TILE)
-        loads[i].wait()
+        coef_col = jnp.broadcast_to(coef[:, here], (HEAD_DIM, TILE)).T
         for h in range(columns // HEAD_DIM):
             lanes = slice(h * HEAD_DIM, (h + 1) * HEAD_DIM)
-            dq[here, lanes] = (dq[here, lanes].astype(jnp.float32) * coef_col[here]).astype(dq.dtype)
+            dq[here, lanes] = (dq_in[here, lanes].astype(jnp.float32) * coef_col).astype(dq.dtype)
         stores[i].start()
     for copy in stores + passed:
         copy.wait()
@@ -309,24 +320,22 @@
 
 def finish(coef, dq, dk, dv):
     hbm = pl.BlockSpec(memory_space=pltpu.HBM)
-    rows = dq.shape[0]
+    vmem = pl.BlockSpec(memory_space=pltpu.VMEM)
     return pl.pallas_call(
         finish_kernel,
         out_shape=tuple(jax.ShapeDtypeStruct(a.shape, a.dtype) for a in (dq, dk, dv)),
-        in_specs=[hbm] * 4,
+        in_specs=[vmem] * 4,
         out_specs=(hbm,) * 3,
-        scratch_shapes=[pltpu.VMEM(coef.shape, jnp.float32), pltpu.VMEM(dq.shape, dq.dtype),
-                        pltpu.SemaphoreType.DMA((3 + 2 * (rows // TILE),))],
-        compiler_params=pltpu.CompilerParams(vmem_limit_bytes=58 * 2**20),
+        scratch_shapes=[pltpu.VMEM(dq.shape, dq.dtype), pltpu.SemaphoreType.DMA((2 + dq.shape[0] // TILE,))],
+        compiler_params=pltpu.CompilerParams(vmem_limit_bytes=32 * 2**20),
         name="finish",
-    )(*in_hbm(coef, dq, dk, dv))
+    )(coef, dq, dk, dv)
 
 
 def solution(mesh):
     blocks, nt = mesh.shape["dp"], mesh.shape["tensor"]
     top = blocks.bit_length() - 1
-    plane_bits, z_lo_bits = (0, top - 2, top - 1), tuple(range(1, top - 2))
-    bits = (plane_bits, z_lo_bits, 2 << len(z_lo_bits))
+    bits = ((0, top - 2, top - 1), tuple(range(1, top - 2)))
 
     def local(query_heads, key_heads, value_heads, logp_grad, logp_new, logp_old, advantage, ratio_caps,
               live_counts, seq_begin, seg_begin, policy_version):

time: 37.3 us -> 29.1 us (0.78)
  Pallas kernels: 35.8 us -> 27.3 us
    pallas_call x1, Pallas kernels: 9.15 us -> 1.17 us  [finish(): pl.pallas_call(finish_kernel, out_shape=tuple((jax.ShapeDtypeStruct(a.sha...]
    pallas_call x1, Pallas kernels: 26.7 us -> 26.1 us  [block(): pl.pallas_call(functools.partial(block_kernel, tokens, plane_bits, line_b...]
where the time goes in v3:
time: 29.1 us; the launch traced here: 28.6 us
  Pallas kernels  27.3 us (94%)
  between operations  1.29 us (4%)
    pallas_call x1, Pallas kernels, block(): pl.pallas_call(functools.partial(block_kernel, tokens, plane_bits, line_b...  26.1 us
    pallas_call x1, Pallas kernels, finish(): pl.pallas_call(finish_kernel, out_shape=tuple((jax.ShapeDtypeStruct(a.sha...  1.17 us

profile of v3, /device:TPU:1, one launch (start us, length us, event | category | flops | bytes accessed | tf_op | source)
XLA Modules:
  0.0 28.6 jit_solution(15629785686364084273)
XLA Ops:
  1.3 26.1 %block.1 = (bf16[512,1024]{1,0:T(8,128)(2,1)S(1)}, bf16[512,128]{1,0:T(8,128)(2,1)S(1)}, bf16[512,128]{1,0:T(8,128)(2,1)S(1)}, f32[1,512]{1,0:T(1,128)S(1)}) custom-call(s32[1]{0:T(128)S(6)} %copy.15.cnt_s, f32[1,64]{1,0:T(1,128)} %bitcast.9, f32[1,64]{1,0:T(1,128)} %bitcast.10, f32[1,64]{1,0:T(1,128)} %bitcast.11, f32[4]{0:T(128)} %caps_hbm.1, ...), custom_call_target="tpu_custom_call" | custom-call | tf_op jit(solution)/shard_map/block/pallas_call | solution.py:274
  27.4 1.2 %finish.1 = (bf16[512,1024]{1,0:T(8,128)(2,1)}, bf16[512,128]{1,0:T(8,128)(2,1)}, bf16[512,128]{1,0:T(8,128)(2,1)}) custom-call(f32[1,512]{1,0:T(1,128)S(1)} %get-tuple-element.7.coef, bf16[512,1024]{1,0:T(8,128)(2,1)S(1)} %get-tuple-element.8.dq_in, bf16[512,128]{1,0:T(8,128)(2,1)S(1)} %get-tuple-element.9.dk_in, bf16[512,128]{1,0:T(8,128)(2,1)S(1)} %get-tuple-element.10.dv_in), custom_call_target="tpu_custom_call" | custom-call | tf_op jit(solution)/shard_map/finish/pallas_call | solution.py:324

commit v4 on v3

--- a/solution.py
+++ b/solution.py
@@ -25,7 +25,7 @@
 def partners(index, bits):
     deltas = flips(index, bits)
     found = []
-    for mask in range(1, 1 << len(bits)):
+    for mask in range((1 << len(bits)) - 1, 0, -1):
         other = index
         for n, delta in enumerate(deltas):
             if mask >> n & 1:
@@ -75,7 +75,7 @@
                  dq, dk_ref, dv_ref, coef_ref,
                  q, k, v, g, cq, cg, probs_t, dscore_t, k_t, bias, same, row_cap, dk_sum, dv_sum,
                  caps_s, seq_ref, seg_ref, ver_ref,
-                 new_v, old_v, adv_v, own_row, rows_in, cnt_row, cnt_rows, part_row, part_rows, total_row,
+                 new_v, old_v, adv_v, own_row, rows_in, cnt_row, cnt_rows, part_row, part_rows,
                  sems, load_sem, send_sem, recv_sem):
     rows, columns = q.shape
     heads = columns // HEAD_DIM
@@ -91,26 +91,14 @@
     plane_peers = [(d, me) for d in partners(dp, plane_bits)]
     half = nt // 2
     far = me >= half
-    near = me < half
-    line = [dp] + partners(dp, line_bits)
-    far_line = [(d, me + half) for d in line]
-    near_line = [(d, me - half) for d in line]
+    across = lax.rem(me + half, nt)
+    line_peers = [(d, across) for d in partners(dp, line_bits)]
+    cross, beside = tensor_peers[:half], tensor_peers[half:]
+    greeted = len(tensor_peers) + len(plane_peers) + len(line_peers)
 
     barrier = pltpu.get_barrier_semaphore()
-
-    def greet(peers):
-        for peer in peers:
-            pl.semaphore_signal(barrier, inc=1, device_id=peer, device_id_type=MESH)
-
-    greet(tensor_peers)
-
-    @pl.when(far)
-    def _():
-        greet(plane_peers)
-
-    @pl.when(near)
-    def _():
-        greet(far_line[1:])
+    for peer in beside + plane_peers + cross + line_peers:
+        pl.semaphore_signal(barrier, inc=1, device_id=peer, device_id_type=MESH)
 
     def start_all(pairs, sem, first):
         copies = [pltpu.make_async_copy(src, dst, sem.at[first + n]) for n, (src, dst) in enumerate(pairs)]
@@ -135,32 +123,25 @@
         span = buffer.at[pl.ds(0, n)]
         pltpu.make_async_copy(span, span, sem).wait()
 
-    def send_rows(signals):
+    def send_own():
         for load in own_in:
             load.wait()
         own_row[0] = jnp.concatenate([new_v[...] - old_v[...], adv_v[...]], axis=1)
-        pl.semaphore_wait(barrier, signals)
+        cnt_row[0] = jnp.full((1, 128), cnt_s[0].astype(f32), f32)
+        pl.semaphore_wait(barrier, greeted)
         for n, peer in enumerate(tensor_peers):
             send(own_row, rows_in.at[pl.ds(n, 1)], 0, peer)
-
-    def send_partial():
         for n, peer in enumerate(plane_peers):
             send(cnt_row, cnt_rows.at[pl.ds(n, 1)], 1, peer)
+
+    def send_partial():
         drain(cnt_rows, len(plane_peers), recv_sem.at[1])
         part = cnt_row[0]
         for n in range(len(plane_peers)):
             part = part + cnt_rows[n]
         part_row[0] = part
-        for n, peer in enumerate(near_line):
+        for n, peer in enumerate(line_peers + [(dp, across)]):
             send(part_row, part_rows.at[pl.ds(n, 1)], 2, peer)
-
-    def send_total():
-        drain(part_rows, len(line), recv_sem.at[2])
-        total = part_rows[0]
-        for n in range(1, len(line)):
-            total = total + part_rows[n]
-        total_row[0] = total
-        send(total_row, total_row, 3, far_line[0])
 
     def head_pair(ref, i, p):
         return jnp.concatenate(
@@ -171,8 +152,7 @@
 
     @pl.when(far)
     def _():
-        cnt_row[0] = jnp.full((1, 128), cnt_s[0].astype(f32), f32)
-        send_rows(len(tensor_peers) + len(plane_peers) + len(line) - 1)
+        send_own()
         send_partial()
 
     for load in small_in:
@@ -210,9 +190,9 @@
             dq[i * TILE:(i + 1) * TILE, h * HEAD_DIM:(h + 1) * HEAD_DIM] = (
                 dq_t[:, h * TILE:(h + 1) * TILE].T.astype(bf16))
 
-    @pl.when(near)
+    @pl.when(jnp.logical_not(far))
     def _():
-        send_rows(len(tensor_peers))
+        send_own()
 
     drain(rows_in, nt - 1, recv_sem.at[0])
     owner_row = lax.broadcasted_iota(jnp.int32, (nt, 128), 0)
@@ -221,9 +201,9 @@
         gathered = jnp.where(owner_row == owners[n], jnp.broadcast_to(rows_in[n], (nt, 128)), gathered)
     coef = row_coefs(tokens, gathered, same[...], row_cap[...], cnt_s[0])
 
-    @pl.when(near)
+    @pl.when(jnp.logical_not(far))
     def _():
-        send_total()
+        send_partial()
 
     coef_col = jnp.broadcast_to(coef, (HEAD_DIM, rows)).T
     for h in range(heads):
@@ -238,26 +218,17 @@
                 [right[i * TILE:(i + 1) * TILE, h * HEAD_DIM:(h + 1) * HEAD_DIM] for i, h in stack], axis=0)
             target[j * TILE:(j + 1) * TILE, :] = jnp.dot(
                 source[j * TILE:(j + 1) * TILE, lanes], stacked, preferred_element_type=f32)
-
-    @pl.when(far)
-    def _():
-        drain(total_row, 1, recv_sem.at[3])
-
-    total = total_row[0]
+    drain(part_rows, len(line_peers) + 1, recv_sem.at[2])
+    total = part_rows[0]
+    for n in range(len(line_peers)):
+        total = total + part_rows[n + 1]
     inverse = jnp.where(total > 0.0, 1.0 / total, 0.0)
     coef_ref[...] = coef * jnp.concatenate([inverse] * (rows // 128), axis=1)
     dv_ref[...] = (dv_sum[...] * inverse).astype(bf16)
     dk_ref[...] = (dk_sum[...] * (inverse * scale)).astype(bf16)
     drain(rows_in, nt - 1, send_sem.at[0])
-
-    @pl.when(far)
-    def _():
-        drain(cnt_rows, len(plane_peers), send_sem.at[1])
-        drain(part_rows, len(line), send_sem.at[2])
-
-    @pl.when(near)
-    def _():
-        drain(total_row, 1, send_sem.at[3])
+    drain(cnt_rows, len(plane_peers), send_sem.at[1])
+    drain(part_rows, len(line_peers) + 1, send_sem.at[2])
 
 
 def block(tokens, bits, nt, cnt, logp_new, logp_old, advantage, caps, seq_begin, seg_begin, version, q, k, v, g):
@@ -289,8 +260,8 @@
             pltpu.VMEM((1, own), f32), pltpu.VMEM((1, own), f32), pltpu.VMEM((1, own), f32),
             pltpu.VMEM((1, 1, 128), f32), pltpu.VMEM((nt - 1, 1, 128), f32),
             pltpu.VMEM((1, 1, 128), f32), pltpu.VMEM((planes - 1, 1, 128), f32),
-            pltpu.VMEM((1, 1, 128), f32), pltpu.VMEM((low, 1, 128), f32), pltpu.VMEM((1, 1, 128), f32),
-            dma((6 + 2 * tiles,)), dma((3,)), dma((4,)), dma((4,)),
+            pltpu.VMEM((1, 1, 128), f32), pltpu.VMEM((low, 1, 128), f32),
+            dma((6 + 2 * tiles,)), dma((3,)), dma((3,)), dma((3,)),
         ],
         compiler_params=pltpu.CompilerParams(
             collective_id=0, has_side_effects=True, vmem_limit_bytes=32 * 2**20),

time: 29.1 us -> 27.6 us (0.948); the launches traced: 28.6 us -> 27.4 us
  Pallas kernels: 27.3 us -> 26.1 us
    pallas_call x1, Pallas kernels: 26.1 us -> 25 us  [block(): pl.pallas_call(functools.partial(block_kernel, tokens, plane_bits, line_b...]
where the time goes in v4:
time: 27.6 us; the launch traced here: 27.4 us
  Pallas kernels  26.1 us (95%)
  between operations  1.29 us (5%)
    pallas_call x1, Pallas kernels, block(): pl.pallas_call(functools.partial(block_kernel, tokens, plane_bits, line_b...  25 us
    pallas_call x1, Pallas kernels, finish(): pl.pallas_call(finish_kernel, out_shape=tuple((jax.ShapeDtypeStruct(a.sha...  1.17 us

profile of v4, /device:TPU:1, one launch (start us, length us, event | category | flops | bytes accessed | tf_op | source)
XLA Modules:
  0.0 27.4 jit_solution(260974123447640413)
XLA Ops:
  1.3 25.0 %block.1 = (bf16[512,1024]{1,0:T(8,128)(2,1)S(1)}, bf16[512,128]{1,0:T(8,128)(2,1)S(1)}, bf16[512,128]{1,0:T(8,128)(2,1)S(1)}, f32[1,512]{1,0:T(1,128)S(1)}) custom-call(s32[1]{0:T(128)S(6)} %copy.15.cnt_s, f32[1,64]{1,0:T(1,128)} %bitcast.9, f32[1,64]{1,0:T(1,128)} %bitcast.10, f32[1,64]{1,0:T(1,128)} %bitcast.11, f32[4]{0:T(128)} %caps_hbm.1, ...), custom_call_target="tpu_custom_call" | custom-call | tf_op jit(solution)/shard_map/block/pallas_call | solution.py:245
  26.2 1.2 %finish.1 = (bf16[512,1024]{1,0:T(8,128)(2,1)}, bf16[512,128]{1,0:T(8,128)(2,1)}, bf16[512,128]{1,0:T(8,128)(2,1)}) custom-call(f32[1,512]{1,0:T(1,128)S(1)} %get-tuple-element.7.coef, bf16[512,1024]{1,0:T(8,128)(2,1)S(1)} %get-tuple-element.8.dq_in, bf16[512,128]{1,0:T(8,128)(2,1)S(1)} %get-tuple-element.9.dk_in, bf16[512,128]{1,0:T(8,128)(2,1)S(1)} %get-tuple-element.10.dv_in), custom_call_target="tpu_custom_call" | custom-call | tf_op jit(solution)/shard_map/finish/pallas_call | solution.py:295

commit v5 on v4

--- a/solution.py
+++ b/solution.py
@@ -73,7 +73,7 @@
 def block_kernel(tokens, plane_bits, line_bits, nt, cnt_s,
                  new_hbm, old_hbm, adv_hbm, caps_hbm, seq_hbm, seg_hbm, ver_hbm, q_hbm, k_hbm, v_hbm, g_hbm,
                  dq, dk_ref, dv_ref, coef_ref,
-                 q, k, v, g, cq, cg, probs_t, dscore_t, k_t, bias, same, row_cap, dk_sum, dv_sum,
+                 q, k, v, g, probs_t, dscore_t, k_t, bias, same, row_cap, dk_sum, dv_sum,
                  caps_s, seq_ref, seg_ref, ver_ref,
                  new_v, old_v, adv_v, own_row, rows_in, cnt_row, cnt_rows, part_row, part_rows,
                  sems, load_sem, send_sem, recv_sem):
@@ -200,24 +200,31 @@
     for n in range(nt - 1):
         gathered = jnp.where(owner_row == owners[n], jnp.broadcast_to(rows_in[n], (nt, 128)), gathered)
     coef = row_coefs(tokens, gathered, same[...], row_cap[...], cnt_s[0])
+    coef_col = jnp.broadcast_to(coef, (HEAD_DIM, rows)).T
+
+    def scaled_stack(ref, i):
+        here = slice(i * TILE, (i + 1) * TILE)
+        return jnp.concatenate(
+            [(ref[here, h * HEAD_DIM:(h + 1) * HEAD_DIM].astype(f32) * coef_col[here]).astype(bf16)
+             for h in range(heads)], axis=0)
+
+    def stacked_products(source, ref, target):
+        for i in reversed(range(tiles)):
+            span = (i + 1) * TILE
+            part = jnp.dot(source[0:span, i * columns:(i + 1) * columns], scaled_stack(ref, i),
+                           preferred_element_type=f32)
+            if i == tiles - 1:
+                target[...] = part
+            else:
+                target[0:span, :] = target[0:span, :] + part
+
+    stacked_products(probs_t, g, dv_sum)
 
     @pl.when(jnp.logical_not(far))
     def _():
         send_partial()
 
-    coef_col = jnp.broadcast_to(coef, (HEAD_DIM, rows)).T
-    for h in range(heads):
-        lanes = slice(h * HEAD_DIM, (h + 1) * HEAD_DIM)
-        cg[:, lanes] = (g[:, lanes].astype(f32) * coef_col).astype(bf16)
-        cq[:, lanes] = (q[:, lanes].astype(f32) * coef_col).astype(bf16)
-    for j in range(tiles):
-        lanes = slice(j * columns, tiles * columns)
-        stack = [(i, h) for i in range(j, tiles) for h in range(heads)]
-        for source, right, target in ((probs_t, cg, dv_sum), (dscore_t, cq, dk_sum)):
-            stacked = jnp.concatenate(
-                [right[i * TILE:(i + 1) * TILE, h * HEAD_DIM:(h + 1) * HEAD_DIM] for i, h in stack], axis=0)
-            target[j * TILE:(j + 1) * TILE, :] = jnp.dot(
-                source[j * TILE:(j + 1) * TILE, lanes], stacked, preferred_element_type=f32)
+    stacked_products(dscore_t, q, dk_sum)
     drain(part_rows, len(line_peers) + 1, recv_sem.at[2])
     total = part_rows[0]
     for n in range(len(line_peers)):
@@ -250,7 +257,6 @@
         out_specs=(vmem,) * 4,
         scratch_shapes=[
             pltpu.VMEM(wide, bf16), pltpu.VMEM(narrow, bf16), pltpu.VMEM(narrow, bf16), pltpu.VMEM(wide, bf16),
-            pltpu.VMEM(wide, bf16), pltpu.VMEM(wide, bf16),
             pltpu.VMEM((rows, tiles * columns), bf16), pltpu.VMEM((rows, tiles * columns), bf16),
             pltpu.VMEM((HEAD_DIM, rows), bf16), pltpu.VMEM((rows, TILE), f32),
             pltpu.VMEM((rows, rows), bf16), pltpu.VMEM((1, rows), f32),

time: 27.6 us -> 27.5 us (level)
  no operation moved by 1% of the time
where the time goes in v5:
time: 27.5 us; the launch traced here: 27.4 us
  Pallas kernels  26.1 us (95%)
  between operations  1.29 us (5%)
    pallas_call x1, Pallas kernels, block(): pl.pallas_call(functools.partial(block_kernel, tokens, plane_bits, line_b...  24.9 us
    pallas_call x1, Pallas kernels, finish(): pl.pallas_call(finish_kernel, out_shape=tuple((jax.ShapeDtypeStruct(a.sha...  1.17 us

profile of v5, /device:TPU:1, one launch (start us, length us, event | category | flops | bytes accessed | tf_op | source)
XLA Modules:
  0.0 27.4 jit_solution(1012278323439067846)
XLA Ops:
  1.3 24.9 %block.1 = (bf16[512,1024]{1,0:T(8,128)(2,1)S(1)}, bf16[512,128]{1,0:T(8,128)(2,1)S(1)}, bf16[512,128]{1,0:T(8,128)(2,1)S(1)}, f32[1,512]{1,0:T(1,128)S(1)}) custom-call(s32[1]{0:T(128)S(6)} %copy.15.cnt_s, f32[1,64]{1,0:T(1,128)} %bitcast.9, f32[1,64]{1,0:T(1,128)} %bitcast.10, f32[1,64]{1,0:T(1,128)} %bitcast.11, f32[4]{0:T(128)} %caps_hbm.1, ...), custom_call_target="tpu_custom_call" | custom-call | tf_op jit(solution)/shard_map/block/pallas_call | solution.py:252
  26.2 1.2 %finish.1 = (bf16[512,1024]{1,0:T(8,128)(2,1)}, bf16[512,128]{1,0:T(8,128)(2,1)}, bf16[512,128]{1,0:T(8,128)(2,1)}) custom-call(f32[1,512]{1,0:T(1,128)S(1)} %get-tuple-element.7.coef, bf16[512,1024]{1,0:T(8,128)(2,1)S(1)} %get-tuple-element.8.dq_in, bf16[512,128]{1,0:T(8,128)(2,1)S(1)} %get-tuple-element.9.dk_in, bf16[512,128]{1,0:T(8,128)(2,1)S(1)} %get-tuple-element.10.dv_in), custom_call_target="tpu_custom_call" | custom-call | tf_op jit(solution)/shard_map/finish/pallas_call | solution.py:301

commit v6 on v5

--- a/solution.py
+++ b/solution.py
@@ -75,7 +75,7 @@
                  dq, dk_ref, dv_ref, coef_ref,
                  q, k, v, g, probs_t, dscore_t, k_t, bias, same, row_cap, dk_sum, dv_sum,
                  caps_s, seq_ref, seg_ref, ver_ref,
-                 new_v, old_v, adv_v, own_row, rows_in, cnt_row, cnt_rows, part_row, part_rows,
+                 new_v, old_v, adv_v, own_row, rows_in, cnt_row, cnt_rows, part_row, part_rows, total_row,
                  sems, load_sem, send_sem, recv_sem):
     rows, columns = q.shape
     heads = columns // HEAD_DIM
@@ -94,11 +94,22 @@
     across = lax.rem(me + half, nt)
     line_peers = [(d, across) for d in partners(dp, line_bits)]
     cross, beside = tensor_peers[:half], tensor_peers[half:]
-    greeted = len(tensor_peers) + len(plane_peers) + len(line_peers)
+    assert nt == len(plane_peers) + 1 == len(line_peers) + 1
+    greeted = 2 * (nt - 1)
 
     barrier = pltpu.get_barrier_semaphore()
-    for peer in beside + plane_peers + cross + line_peers:
-        pl.semaphore_signal(barrier, inc=1, device_id=peer, device_id_type=MESH)
+
+    def greet(peers):
+        for peer in peers:
+            pl.semaphore_signal(barrier, inc=1, device_id=peer, device_id_type=MESH)
+
+    @pl.when(far)
+    def _():
+        greet(beside + cross)
+
+    @pl.when(jnp.logical_not(far))
+    def _():
+        greet(cross + line_peers + plane_peers + beside)
 
     def start_all(pairs, sem, first):
         copies = [pltpu.make_async_copy(src, dst, sem.at[first + n]) for n, (src, dst) in enumerate(pairs)]
@@ -123,25 +134,40 @@
         span = buffer.at[pl.ds(0, n)]
         pltpu.make_async_copy(span, span, sem).wait()
 
-    def send_own():
+    def send_rows(first, last):
+        for n in range(first, last):
+            send(own_row, rows_in.at[pl.ds(n, 1)], 0, tensor_peers[n])
+
+    def ready_to_send():
         for load in own_in:
             load.wait()
         own_row[0] = jnp.concatenate([new_v[...] - old_v[...], adv_v[...]], axis=1)
+        pl.semaphore_wait(barrier, greeted)
+
+    def far_sends():
         cnt_row[0] = jnp.full((1, 128), cnt_s[0].astype(f32), f32)
-        pl.semaphore_wait(barrier, greeted)
-        for n, peer in enumerate(tensor_peers):
-            send(own_row, rows_in.at[pl.ds(n, 1)], 0, peer)
+        ready_to_send()
+        send_rows(0, half)
+        for n, peer in enumerate(line_peers + [(dp, across)]):
+            send(cnt_row, cnt_rows.at[pl.ds(n, 1)], 1, peer)
+        send_rows(half, nt - 1)
+
+    def send_partial():
+        drain(cnt_rows, len(line_peers) + 1, recv_sem.at[1])
+        part = cnt_rows[0]
+        for n in range(len(line_peers)):
+            part = part + cnt_rows[n + 1]
+        part_row[0] = part
         for n, peer in enumerate(plane_peers):
-            send(cnt_row, cnt_rows.at[pl.ds(n, 1)], 1, peer)
-
-    def send_partial():
-        drain(cnt_rows, len(plane_peers), recv_sem.at[1])
-        part = cnt_row[0]
+            send(part_row, part_rows.at[pl.ds(n, 1)], 2, peer)
+
+    def send_total():
+        drain(part_rows, len(plane_peers), recv_sem.at[2])
+        total = part_row[0]
         for n in range(len(plane_peers)):
-            part = part + cnt_rows[n]
-        part_row[0] = part
-        for n, peer in enumerate(line_peers + [(dp, across)]):
-            send(part_row, part_rows.at[pl.ds(n, 1)], 2, peer)
+            total = total + part_rows[n]
+        total_row[0] = total
+        send(total_row, total_row, 3, (dp, across))
 
     def head_pair(ref, i, p):
         return jnp.concatenate(
@@ -152,8 +178,7 @@
 
     @pl.when(far)
     def _():
-        send_own()
-        send_partial()
+        far_sends()
 
     for load in small_in:
         load.wait()
@@ -192,7 +217,8 @@
 
     @pl.when(jnp.logical_not(far))
     def _():
-        send_own()
+        ready_to_send()
+        send_rows(0, nt - 1)
 
     drain(rows_in, nt - 1, recv_sem.at[0])
     owner_row = lax.broadcasted_iota(jnp.int32, (nt, 128), 0)
@@ -218,24 +244,36 @@
             else:
                 target[0:span, :] = target[0:span, :] + part
 
+    @pl.when(jnp.logical_not(far))
+    def _():
+        send_partial()
+
     stacked_products(probs_t, g, dv_sum)
-
-    @pl.when(jnp.logical_not(far))
-    def _():
-        send_partial()
-
     stacked_products(dscore_t, q, dk_sum)
-    drain(part_rows, len(line_peers) + 1, recv_sem.at[2])
-    total = part_rows[0]
-    for n in range(len(line_peers)):
-        total = total + part_rows[n + 1]
+
+    @pl.when(jnp.logical_not(far))
+    def _():
+        send_total()
+
+    @pl.when(far)
+    def _():
+        drain(total_row, 1, recv_sem.at[3])
+
+    total = total_row[0]
     inverse = jnp.where(total > 0.0, 1.0 / total, 0.0)
     coef_ref[...] = coef * jnp.concatenate([inverse] * (rows // 128), axis=1)
     dv_ref[...] = (dv_sum[...] * inverse).astype(bf16)
     dk_ref[...] = (dk_sum[...] * (inverse * scale)).astype(bf16)
     drain(rows_in, nt - 1, send_sem.at[0])
-    drain(cnt_rows, len(plane_peers), send_sem.at[1])
-    drain(part_rows, len(line_peers) + 1, send_sem.at[2])
+
+    @pl.when(far)
+    def _():
+        drain(cnt_rows, len(line_peers) + 1, send_sem.at[1])
+
+    @pl.when(jnp.logical_not(far))
+    def _():
+        drain(part_rows, len(plane_peers), send_sem.at[2])
+        drain(total_row, 1, send_sem.at[3])
 
 
 def block(tokens, bits, nt, cnt, logp_new, logp_old, advantage, caps, seq_begin, seg_begin, version, q, k, v, g):
@@ -265,9 +303,9 @@
             pltpu.VMEM((1, rows), i32), pltpu.VMEM((1, rows), i32), pltpu.VMEM((1, rows), i32),
             pltpu.VMEM((1, own), f32), pltpu.VMEM((1, own), f32), pltpu.VMEM((1, own), f32),
             pltpu.VMEM((1, 1, 128), f32), pltpu.VMEM((nt - 1, 1, 128), f32),
-            pltpu.VMEM((1, 1, 128), f32), pltpu.VMEM((planes - 1, 1, 128), f32),
             pltpu.VMEM((1, 1, 128), f32), pltpu.VMEM((low, 1, 128), f32),
-            dma((6 + 2 * tiles,)), dma((3,)), dma((3,)), dma((3,)),
+            pltpu.VMEM((1, 1, 128), f32), pltpu.VMEM((planes - 1, 1, 128), f32), pltpu.VMEM((1, 1, 128), f32),
+            dma((6 + 2 * tiles,)), dma((3,)), dma((4,)), dma((4,)),
         ],
         compiler_params=pltpu.CompilerParams(
             collective_id=0, has_side_effects=True, vmem_limit_bytes=32 * 2**20),

time: 27.5 us -> 30.2 us (1.098)
  the two profiles are of different devices: /device:TPU:1 before, /device:TPU:480 now
where the time goes in v6:
time: 30.2 us; the launch traced here: 30 us
  Pallas kernels  28.7 us (95%)
  between operations  1.29 us (4%)
    pallas_call x1, Pallas kernels, block(): pl.pallas_call(functools.partial(block_kernel, tokens, plane_bits, line_b...  27.6 us
    pallas_call x1, Pallas kernels, finish(): pl.pallas_call(finish_kernel, out_shape=tuple((jax.ShapeDtypeStruct(a.sha...  1.17 us

profile of v6, /device:TPU:480, one launch (start us, length us, event | category | flops | bytes accessed | tf_op | source)
XLA Modules:
  0.0 30.0 jit_solution(17110594412449548616)
XLA Ops:
  1.3 27.6 %block.1 = (bf16[512,1024]{1,0:T(8,128)(2,1)S(1)}, bf16[512,128]{1,0:T(8,128)(2,1)S(1)}, bf16[512,128]{1,0:T(8,128)(2,1)S(1)}, f32[1,512]{1,0:T(1,128)S(1)}) custom-call(s32[1]{0:T(128)S(6)} %copy.15.cnt_s, f32[1,64]{1,0:T(1,128)} %bitcast.9, f32[1,64]{1,0:T(1,128)} %bitcast.10, f32[1,64]{1,0:T(1,128)} %bitcast.11, f32[4]{0:T(128)} %caps_hbm.1, ...), custom_call_target="tpu_custom_call" | custom-call | tf_op jit(solution)/shard_map/block/pallas_call | solution.py:290
  28.8 1.2 %finish.1 = (bf16[512,1024]{1,0:T(8,128)(2,1)}, bf16[512,128]{1,0:T(8,128)(2,1)}, bf16[512,128]{1,0:T(8,128)(2,1)}) custom-call(f32[1,512]{1,0:T(1,128)S(1)} %get-tuple-element.7.coef, bf16[512,1024]{1,0:T(8,128)(2,1)S(1)} %get-tuple-element.8.dq_in, bf16[512,128]{1,0:T(8,128)(2,1)S(1)} %get-tuple-element.9.dk_in, bf16[512,128]{1,0:T(8,128)(2,1)S(1)} %get-tuple-element.10.dv_in), custom_call_target="tpu_custom_call" | custom-call | tf_op jit(solution)/shard_map/finish/pallas_call | solution.py:339

commit v7 on v5

--- a/solution.py
+++ b/solution.py
@@ -123,16 +123,20 @@
         span = buffer.at[pl.ds(0, n)]
         pltpu.make_async_copy(span, span, sem).wait()
 
+    def send_rows(first, last):
+        for n in range(first, last):
+            send(own_row, rows_in.at[pl.ds(n, 1)], 0, tensor_peers[n])
+
     def send_own():
         for load in own_in:
             load.wait()
         own_row[0] = jnp.concatenate([new_v[...] - old_v[...], adv_v[...]], axis=1)
         cnt_row[0] = jnp.full((1, 128), cnt_s[0].astype(f32), f32)
         pl.semaphore_wait(barrier, greeted)
-        for n, peer in enumerate(tensor_peers):
-            send(own_row, rows_in.at[pl.ds(n, 1)], 0, peer)
+        send_rows(0, half)
         for n, peer in enumerate(plane_peers):
             send(cnt_row, cnt_rows.at[pl.ds(n, 1)], 1, peer)
+        send_rows(half, nt - 1)
 
     def send_partial():
         drain(cnt_rows, len(plane_peers), recv_sem.at[1])
@@ -193,6 +197,7 @@
     @pl.when(jnp.logical_not(far))
     def _():
         send_own()
+        send_partial()
 
     drain(rows_in, nt - 1, recv_sem.at[0])
     owner_row = lax.broadcasted_iota(jnp.int32, (nt, 128), 0)
@@ -219,11 +224,6 @@
                 target[0:span, :] = target[0:span, :] + part
 
     stacked_products(probs_t, g, dv_sum)
-
-    @pl.when(jnp.logical_not(far))
-    def _():
-        send_partial()
-
     stacked_products(dscore_t, q, dk_sum)
     drain(part_rows, len(line_peers) + 1, recv_sem.at[2])
     total = part_rows[0]
@@ -312,7 +312,7 @@
 def solution(mesh):
     blocks, nt = mesh.shape["dp"], mesh.shape["tensor"]
     top = blocks.bit_length() - 1
-    bits = ((0, top - 2, top - 1), tuple(range(1, top - 2)))
+    bits = ((0,), tuple(range(1, top)))
 
     def local(query_heads, key_heads, value_heads, logp_grad, logp_new, logp_old, advantage, ratio_caps,
               live_counts, seq_begin, seg_begin, policy_version):

time: 27.5 us -> 26.4 us (0.960)
  Pallas kernels: 26.1 us -> 25 us
    pallas_call x1, Pallas kernels: 24.9 us -> 23.8 us  [block(): pl.pallas_call(functools.partial(block_kernel, tokens, plane_bits, line_b...]
where the time goes in v7:
time: 26.4 us; the launch traced here: 26.3 us
  Pallas kernels  25 us (95%)
  between operations  1.29 us (5%)
    pallas_call x1, Pallas kernels, block(): pl.pallas_call(functools.partial(block_kernel, tokens, plane_bits, line_b...  23.8 us
    pallas_call x1, Pallas kernels, finish(): pl.pallas_call(finish_kernel, out_shape=tuple((jax.ShapeDtypeStruct(a.sha...  1.17 us

profile of v7, /device:TPU:1, one launch (start us, length us, event | category | flops | bytes accessed | tf_op | source)
XLA Modules:
  0.0 26.3 jit_solution(3212856521645390145)
XLA Ops:
  1.3 23.8 %block.1 = (bf16[512,1024]{1,0:T(8,128)(2,1)S(1)}, bf16[512,128]{1,0:T(8,128)(2,1)S(1)}, bf16[512,128]{1,0:T(8,128)(2,1)S(1)}, f32[1,512]{1,0:T(1,128)S(1)}) custom-call(s32[1]{0:T(128)S(6)} %copy.15.cnt_s, f32[1,64]{1,0:T(1,128)} %bitcast.9, f32[1,64]{1,0:T(1,128)} %bitcast.10, f32[1,64]{1,0:T(1,128)} %bitcast.11, f32[4]{0:T(128)} %caps_hbm.1, ...), custom_call_target="tpu_custom_call" | custom-call | tf_op jit(solution)/shard_map/block/pallas_call | solution.py:252
  25.1 1.2 %finish.1 = (bf16[512,1024]{1,0:T(8,128)(2,1)}, bf16[512,128]{1,0:T(8,128)(2,1)}, bf16[512,128]{1,0:T(8,128)(2,1)}) custom-call(f32[1,512]{1,0:T(1,128)S(1)} %get-tuple-element.7.coef, bf16[512,1024]{1,0:T(8,128)(2,1)S(1)} %get-tuple-element.8.dq_in, bf16[512,128]{1,0:T(8,128)(2,1)S(1)} %get-tuple-element.9.dk_in, bf16[512,128]{1,0:T(8,128)(2,1)S(1)} %get-tuple-element.10.dv_in), custom_call_target="tpu_custom_call" | custom-call | tf_op jit(solution)/shard_map/finish/pallas_call | solution.py:301

commit v8 on v7

--- a/solution.py
+++ b/solution.py
@@ -70,12 +70,12 @@
     return jnp.where(live, -adv * weight * tokens, 0.0)
 
 
-def block_kernel(tokens, plane_bits, line_bits, nt, cnt_s,
+def block_kernel(tokens, bits, nt, cnt_s,
                  new_hbm, old_hbm, adv_hbm, caps_hbm, seq_hbm, seg_hbm, ver_hbm, q_hbm, k_hbm, v_hbm, g_hbm,
                  dq, dk_ref, dv_ref, coef_ref,
                  q, k, v, g, probs_t, dscore_t, k_t, bias, same, row_cap, dk_sum, dv_sum,
                  caps_s, seq_ref, seg_ref, ver_ref,
-                 new_v, old_v, adv_v, own_row, rows_in, cnt_row, cnt_rows, part_row, part_rows,
+                 new_v, old_v, adv_v, own_row, rows_in, cnt_row, cnt_rows, part_row, part_rows, total_row,
                  sems, load_sem, send_sem, recv_sem):
     rows, columns = q.shape
     heads = columns // HEAD_DIM
@@ -88,17 +88,29 @@
     me = lax.axis_index("tensor")
     owners = partners(me, range(nt.bit_length() - 1))
     tensor_peers = [(dp, t) for t in owners]
-    plane_peers = [(d, me) for d in partners(dp, plane_bits)]
     half = nt // 2
     far = me >= half
+    near = jnp.logical_not(far)
     across = lax.rem(me + half, nt)
-    line_peers = [(d, across) for d in partners(dp, line_bits)]
     cross, beside = tensor_peers[:half], tensor_peers[half:]
-    greeted = len(tensor_peers) + len(plane_peers) + len(line_peers)
+    own_cross = [(dp, across)]
+    far_bits, near_bits = bits
+    far_plane, near_plane = ([(d, me) for d in partners(dp, part[0])] for part in (far_bits, near_bits))
+    far_line, near_line = ([(d, across) for d in partners(dp, part[1])] for part in (far_bits, near_bits))
 
     barrier = pltpu.get_barrier_semaphore()
-    for peer in beside + plane_peers + cross + line_peers:
-        pl.semaphore_signal(barrier, inc=1, device_id=peer, device_id_type=MESH)
+
+    def greet(peers):
+        for peer in peers:
+            pl.semaphore_signal(barrier, inc=1, device_id=peer, device_id_type=MESH)
+
+    @pl.when(far)
+    def _():
+        greet(beside + far_plane + cross + near_line)
+
+    @pl.when(near)
+    def _():
+        greet(cross + far_line + near_plane + beside)
 
     def start_all(pairs, sem, first):
         copies = [pltpu.make_async_copy(src, dst, sem.at[first + n]) for n, (src, dst) in enumerate(pairs)]
@@ -127,25 +139,36 @@
         for n in range(first, last):
             send(own_row, rows_in.at[pl.ds(n, 1)], 0, tensor_peers[n])
 
-    def send_own():
+    def send_own(plane, line):
         for load in own_in:
             load.wait()
         own_row[0] = jnp.concatenate([new_v[...] - old_v[...], adv_v[...]], axis=1)
         cnt_row[0] = jnp.full((1, 128), cnt_s[0].astype(f32), f32)
-        pl.semaphore_wait(barrier, greeted)
+        pl.semaphore_wait(barrier, nt - 1 + len(plane) + len(line))
         send_rows(0, half)
-        for n, peer in enumerate(plane_peers):
+        for n, peer in enumerate(plane):
             send(cnt_row, cnt_rows.at[pl.ds(n, 1)], 1, peer)
         send_rows(half, nt - 1)
 
-    def send_partial():
-        drain(cnt_rows, len(plane_peers), recv_sem.at[1])
+    def send_partial(plane, line):
+        drain(cnt_rows, len(plane), recv_sem.at[1])
         part = cnt_row[0]
-        for n in range(len(plane_peers)):
+        for n in range(len(plane)):
             part = part + cnt_rows[n]
         part_row[0] = part
-        for n, peer in enumerate(line_peers + [(dp, across)]):
+        for n, peer in enumerate(line + own_cross):
             send(part_row, part_rows.at[pl.ds(n, 1)], 2, peer)
+
+    def sum_total(line):
+        drain(part_rows, len(line) + 1, recv_sem.at[2])
+        total = part_rows[0]
+        for n in range(len(line)):
+            total = total + part_rows[n + 1]
+        total_row[0] = total
+
+    def drain_sends(plane, line):
+        drain(cnt_rows, len(plane), send_sem.at[1])
+        drain(part_rows, len(line) + 1, send_sem.at[2])
 
     def head_pair(ref, i, p):
         return jnp.concatenate(
@@ -156,8 +179,8 @@
 
     @pl.when(far)
     def _():
-        send_own()
-        send_partial()
+        send_own(far_plane, far_line)
+        send_partial(far_plane, far_line)
 
     for load in small_in:
         load.wait()
@@ -194,10 +217,9 @@
             dq[i * TILE:(i + 1) * TILE, h * HEAD_DIM:(h + 1) * HEAD_DIM] = (
                 dq_t[:, h * TILE:(h + 1) * TILE].T.astype(bf16))
 
-    @pl.when(jnp.logical_not(far))
-    def _():
-        send_own()
-        send_partial()
+    @pl.when(near)
+    def _():
+        send_own(near_plane, near_line)
 
     drain(rows_in, nt - 1, recv_sem.at[0])
     owner_row = lax.broadcasted_iota(jnp.int32, (nt, 128), 0)
@@ -224,33 +246,49 @@
                 target[0:span, :] = target[0:span, :] + part
 
     stacked_products(probs_t, g, dv_sum)
+
+    @pl.when(near)
+    def _():
+        send_partial(near_plane, near_line)
+
     stacked_products(dscore_t, q, dk_sum)
-    drain(part_rows, len(line_peers) + 1, recv_sem.at[2])
-    total = part_rows[0]
-    for n in range(len(line_peers)):
-        total = total + part_rows[n + 1]
+
+    @pl.when(near)
+    def _():
+        sum_total(far_line)
+
+    @pl.when(far)
+    def _():
+        sum_total(near_line)
+
+    total = total_row[0]
     inverse = jnp.where(total > 0.0, 1.0 / total, 0.0)
     coef_ref[...] = coef * jnp.concatenate([inverse] * (rows // 128), axis=1)
     dv_ref[...] = (dv_sum[...] * inverse).astype(bf16)
     dk_ref[...] = (dk_sum[...] * (inverse * scale)).astype(bf16)
     drain(rows_in, nt - 1, send_sem.at[0])
-    drain(cnt_rows, len(plane_peers), send_sem.at[1])
-    drain(part_rows, len(line_peers) + 1, send_sem.at[2])
+
+    @pl.when(far)
+    def _():
+        drain_sends(far_plane, far_line)
+
+    @pl.when(near)
+    def _():
+        drain_sends(near_plane, near_line)
 
 
 def block(tokens, bits, nt, cnt, logp_new, logp_old, advantage, caps, seq_begin, seg_begin, version, q, k, v, g):
-    plane_bits, line_bits = bits
     rows, columns = q.shape
     own = logp_new.shape[0]
     tiles = rows // TILE
-    planes, low = 1 << len(plane_bits), 1 << len(line_bits)
+    planes, low = 1 << max(len(part[0]) for part in bits), 1 << max(len(part[1]) for part in bits)
     bf16, f32, i32 = jnp.bfloat16, jnp.float32, jnp.int32
     hbm = pl.BlockSpec(memory_space=pltpu.HBM)
     vmem = pl.BlockSpec(memory_space=pltpu.VMEM)
     wide, narrow = (rows, columns), (rows, HEAD_DIM)
     dma = pltpu.SemaphoreType.DMA
     return pl.pallas_call(
-        functools.partial(block_kernel, tokens, plane_bits, line_bits, nt),
+        functools.partial(block_kernel, tokens, bits, nt),
         out_shape=(jax.ShapeDtypeStruct(wide, bf16), jax.ShapeDtypeStruct(narrow, bf16),
                    jax.ShapeDtypeStruct(narrow, bf16), jax.ShapeDtypeStruct((1, rows), f32)),
         in_specs=[pl.BlockSpec(memory_space=pltpu.SMEM)] + [hbm] * 11,
@@ -266,7 +304,7 @@
             pltpu.VMEM((1, own), f32), pltpu.VMEM((1, own), f32), pltpu.VMEM((1, own), f32),
             pltpu.VMEM((1, 1, 128), f32), pltpu.VMEM((nt - 1, 1, 128), f32),
             pltpu.VMEM((1, 1, 128), f32), pltpu.VMEM((planes - 1, 1, 128), f32),
-            pltpu.VMEM((1, 1, 128), f32), pltpu.VMEM((low, 1, 128), f32),
+            pltpu.VMEM((1, 1, 128), f32), pltpu.VMEM((low, 1, 128), f32), pltpu.VMEM((1, 1, 128), f32),
             dma((6 + 2 * tiles,)), dma((3,)), dma((3,)), dma((3,)),
         ],
         compiler_params=pltpu.CompilerParams(
@@ -312,7 +350,7 @@
 def solution(mesh):
     blocks, nt = mesh.shape["dp"], mesh.shape["tensor"]
     top = blocks.bit_length() - 1
-    bits = ((0,), tuple(range(1, top)))
+    bits = (((0,), tuple(range(1, top))), ((0, top - 2, top - 1), tuple(range(1, top - 2))))
 
     def local(query_heads, key_heads, value_heads, logp_grad, logp_new, logp_old, advantage, ratio_caps,
               live_counts, seq_begin, seg_begin, policy_version):

time: 26.4 us -> 28.6 us (1.083)
  the two profiles are of different devices: /device:TPU:1 before, /device:TPU:480 now
where the time goes in v8:
time: 28.6 us; the launch traced here: 28.5 us
  Pallas kernels  27.2 us (95%)
  between operations  1.29 us (5%)
    pallas_call x1, Pallas kernels, block(): pl.pallas_call(functools.partial(block_kernel, tokens, bits, nt), out_sha...  26 us
    pallas_call x1, Pallas kernels, finish(): pl.pallas_call(finish_kernel, out_shape=tuple((jax.ShapeDtypeStruct(a.sha...  1.17 us

profile of v8, /device:TPU:480, one launch (start us, length us, event | category | flops | bytes accessed | tf_op | source)
XLA Modules:
  0.0 28.5 jit_solution(476089496829922231)
XLA Ops:
  1.3 26.0 %block.1 = (bf16[512,1024]{1,0:T(8,128)(2,1)S(1)}, bf16[512,128]{1,0:T(8,128)(2,1)S(1)}, bf16[512,128]{1,0:T(8,128)(2,1)S(1)}, f32[1,512]{1,0:T(1,128)S(1)}) custom-call(s32[1]{0:T(128)S(6)} %copy.15.cnt_s, f32[1,64]{1,0:T(1,128)} %bitcast.9, f32[1,64]{1,0:T(1,128)} %bitcast.10, f32[1,64]{1,0:T(1,128)} %bitcast.11, f32[4]{0:T(128)} %caps_hbm.1, ...), custom_call_target="tpu_custom_call" | custom-call | tf_op jit(solution)/shard_map/block/pallas_call | solution.py:290
  27.3 1.2 %finish.1 = (bf16[512,1024]{1,0:T(8,128)(2,1)}, bf16[512,128]{1,0:T(8,128)(2,1)}, bf16[512,128]{1,0:T(8,128)(2,1)}) custom-call(f32[1,512]{1,0:T(1,128)S(1)} %get-tuple-element.7.coef, bf16[512,1024]{1,0:T(8,128)(2,1)S(1)} %get-tuple-element.8.dq_in, bf16[512,128]{1,0:T(8,128)(2,1)S(1)} %get-tuple-element.9.dk_in, bf16[512,128]{1,0:T(8,128)(2,1)S(1)} %get-tuple-element.10.dv_in), custom_call_target="tpu_custom_call" | custom-call | tf_op jit(solution)/shard_map/finish/pallas_call | solution.py:339
